TPU v7x, 512 devices: a whole 4x4x16 slice. The times are simulated.
512 devices in a mesh: fsdp: 2 (over z_hi), seq: 32 (over x, y, core), tp: 8 (over z_lo).
Axes of the slice: x: 4, y: 4, z: 16 (z_hi: 2, z_lo: 8; z = z_hi * 8 + z_lo), core: 2. Of those that a mesh axis runs over, the one named last changes fastest.
Arguments:
- tokens: bfloat16 [16384, 8192], P(('fsdp', 'seq', 'tp')), may hold values from -6 to 6
- proj_mean: bfloat16 [8192, 4096], P(('fsdp', 'seq'), 'tp'), may hold values from -0.0625 to 0.0625
- proj_devs: bfloat16 [4, 8192, 4096], P(None, ('fsdp', 'seq'), 'tp'), may hold values from -0.0625 to 0.0625
- bc_mean: bfloat16 [8192, 2, 1024], P(('fsdp', 'seq'), None, 'tp'), may hold values from -0.0625 to 0.0625
- bc_devs: bfloat16 [4, 8192, 2, 1024], P(None, ('fsdp', 'seq'), None, 'tp'), may hold values from -0.0625 to 0.0625
- swag_coef: float32 [4], replicated, may hold values from -4 to 4
- dt_weight: bfloat16 [8192, 64], P(('fsdp', 'seq'), 'tp'), may hold values from -0.0625 to 0.0625
- dt_bias: float32 [64], P('tp'), may hold values from -12 to -2, as said below
- decay_rate: float32 [64], P('tp'), may hold values from 0 to 16, as said below
- skip_gain: float32 [64], P('tp'), may hold values from 0.5 to 1.5
- conv_proj: float32 [4, 4096], P(None, 'tp'), may hold values from -3 to 3
- conv_bc: float32 [4, 2, 1024], P(None, None, 'tp'), may hold values from -1.5 to 1.5
Outputs:
- ssm_out: bfloat16 [16384, 4096], P(('fsdp', 'seq'), 'tp')
Inputs may be any that keep to these rules, and one draw needn't show every extreme that they name: `dt_bias`: every bias is the inverse softplus of a positive step size. `decay_rate`: every rate is positive.
All inputs are finite; a program needn't handle non-finite values.
Results may differ from a plain program's by a relative error of at most 0.0059.
Values may be sent and summed in bfloat16 or wider, within the bound.
A program may use at most 64 MiB of HBM per device.

v0:
```python
import jax
import jax.numpy as jnp
from jax import lax
from jax.sharding import PartitionSpec as P

P_SIZE = 64
N = 128
CONV = 4
SPAN = 128


def shifted(shard, axis, by):
    count = lax.axis_size(axis)
    pairs = [(i, i + by) for i in range(count) if 0 <= i + by < count]
    return lax.ppermute(shard, axis, pairs)


def prefix(part, axis, combine, identity):
    place = lax.axis_index(axis)
    gathered = jax.tree.map(lambda a: lax.all_gather(a, axis), part)
    state = jax.tree.map(lambda a, e: jnp.zeros_like(a) + jnp.asarray(e, a.dtype), part, identity)

    def one(hop, state):
        return combine(
            state, jax.tree.map(lambda a: lax.dynamic_index_in_dim(a, hop, 0, False), gathered)
        )

    return lax.fori_loop(0, place, one, state)


def sampled(mean_part, dev_part, swag_coef):
    factor = (2.0 * (dev_part.shape[0] - 1)) ** (-0.5)
    accum = mean_part.astype(jnp.float32)
    for member in range(dev_part.shape[0]):
        accum = accum + factor * swag_coef[member] * dev_part[member].astype(jnp.float32)
    return accum.astype(jnp.bfloat16)


def combine(former, latter):
    return (former[0] * latter[0], latter[0][:, None, None] * former[1] + latter[1])


def body(
    tokens,
    proj_mean,
    proj_devs,
    bc_mean,
    bc_devs,
    swag_coef,
    dt_weight,
    dt_bias,
    decay_rate,
    skip_gain,
    conv_proj,
    conv_bc,
):
    heads_here = decay_rate.shape[0]
    groups_here = bc_mean.shape[2] // N
    width_x = proj_mean.shape[1]
    width_bc = 2 * bc_mean.shape[2]
    rows_all = lax.all_gather(tokens, "tp", axis=0, tiled=True)
    tok_count = rows_all.shape[0]
    weight_x = sampled(proj_mean, proj_devs, swag_coef)
    weight_bc = sampled(bc_mean, bc_devs, swag_coef).reshape(bc_mean.shape[0], width_bc)
    weight_all = jnp.concatenate([weight_x, weight_bc], axis=1)
    projected = jnp.dot(
        rows_all,
        lax.all_gather(weight_all, ("fsdp", "seq"), axis=0, tiled=True),
        preferred_element_type=jnp.float32,
    ).astype(jnp.bfloat16)
    step_size = jax.nn.softplus(
        jnp.dot(
            rows_all,
            lax.all_gather(dt_weight, ("fsdp", "seq"), axis=0, tiled=True),
            preferred_element_type=jnp.float32,
        )
        + dt_bias
    )
    rim_rows = shifted(projected[tok_count - (CONV - 1) :], "seq", 1)
    padded = jnp.concatenate([rim_rows, projected], axis=0).astype(jnp.float32)
    kernel = jnp.concatenate([conv_proj, conv_bc.reshape(CONV, width_bc)], axis=1)
    conv_sum = kernel[0] * padded[0:tok_count]
    for offset in range(1, CONV):
        conv_sum = conv_sum + kernel[offset] * padded[offset : offset + tok_count]
    conved = jax.nn.silu(conv_sum).astype(jnp.bfloat16)
    blocks = tok_count // SPAN
    per_group = heads_here // groups_here
    values = conved[:, :width_x].reshape(blocks, SPAN, heads_here, P_SIZE)
    keys_b = conved[:, width_x : width_x + width_bc // 2].reshape(blocks, SPAN, groups_here, N)
    reads_c = conved[:, width_x + width_bc // 2 :].reshape(blocks, SPAN, groups_here, N)
    steps_b = step_size.reshape(blocks, SPAN, heads_here)
    cum_log = jnp.cumsum(-steps_b * decay_rate, axis=1)
    last_cum = cum_log[:, SPAN - 1 :, :]
    scaled = (
        values.astype(jnp.float32) * (jnp.exp(last_cum - cum_log) * steps_b)[..., None]
    ).astype(jnp.bfloat16)
    keys_h = jnp.repeat(keys_b, per_group, axis=2)
    states = jnp.einsum("bshn,bshp->bhnp", keys_h, scaled, preferred_element_type=jnp.float32)
    block_decay = jnp.exp(last_cum[:, 0, :])
    total_decay = block_decay[0]
    total_state = states[0]
    member = 1
    total_decay, total_state = combine(
        (total_decay, total_state), (block_decay[member], states[member])
    )
    incoming = prefix(
        (total_decay, total_state),
        "seq",
        combine,
        (jnp.ones((heads_here,), jnp.float32), jnp.zeros((heads_here, N, P_SIZE), jnp.float32)),
    )
    scores = jnp.einsum("bqgn,bsgn->bgqs", reads_c, keys_b, preferred_element_type=jnp.float32)
    scores = jnp.repeat(scores, per_group, axis=1)
    causal_mask = jnp.tril(jnp.ones((SPAN, SPAN), bool))
    later_cum = jnp.transpose(cum_log, (0, 2, 1))
    cum_gaps = later_cum[:, :, :, None] - later_cum[:, :, None, :]
    decays = jnp.where(causal_mask, jnp.exp(jnp.minimum(cum_gaps, 0.0)), 0.0)
    weights = (scores * decays * jnp.transpose(steps_b, (0, 2, 1))[:, :, None, :]).astype(
        jnp.bfloat16
    )
    inner_part = jnp.einsum("bhqs,bshp->bqhp", weights, values, preferred_element_type=jnp.float32)
    carried = incoming[1]
    entering = []
    for member in range(blocks):
        entering.append(carried)
        carried = block_decay[member][:, None, None] * carried + states[member]
    entering_bf = jnp.stack(entering).astype(jnp.bfloat16)
    reads_h = jnp.repeat(reads_c, per_group, axis=2)
    outer_part = jnp.exp(cum_log)[..., None] * jnp.einsum(
        "bqhn,bhnp->bqhp", reads_h, entering_bf, preferred_element_type=jnp.float32
    )
    result = inner_part + outer_part + skip_gain[:, None] * values.astype(jnp.float32)
    return result.reshape(tok_count, width_x).astype(jnp.bfloat16)


def solution(mesh):
    return jax.shard_map(
        body,
        mesh=mesh,
        in_specs=(
            P(("fsdp", "seq", "tp"), None),
            P(("fsdp", "seq"), "tp"),
            P(None, ("fsdp", "seq"), "tp"),
            P(("fsdp", "seq"), None, "tp"),
            P(None, ("fsdp", "seq"), None, "tp"),
            P(),
            P(("fsdp", "seq"), "tp"),
            P("tp"),
            P("tp"),
            P("tp"),
            P(None, "tp"),
            P(None, None, "tp"),
        ),
        out_specs=P(("fsdp", "seq"), "tp"),
        check_vma=False,
    )
```

profile of v0, /device:TPU:31, one launch (start us, length us, event | category | flops | bytes accessed | tf_op | source)
XLA Modules:
  0.0 457.1 jit_solution(740776401347183553)
XLA Ops:
  6.5 0.7 all-gather.7.cloned.1.call-update
  7.3 1.5 fusion.31
  11.3 1.2 fusion.26
  12.5 1.3 fusion.21
  13.8 0.7 pad_maximum_fusion
  14.6 148.3 %all_gather.19 = bf16[8192,8]{0,1:T(8,128)(2,1)S(1)} all-gather(bf16[128,8]{0,1:T(8,128)(2,1)} %param.20), channel_id=1, replica_groups=mesh['fsdp'=2,'seq'=32,'tp'=8] {'fsdp','seq'}, dimensions={0}, use_global_device_ids=true | all-gather | bytes 133120 | tf_op jit(solution)/shard_map/all_gather | solution.py:74
  162.8 0.7 constant_dynamic-update-slice_fusion.1
  163.5 0.7 constant_dynamic-update-slice_fusion
  164.3 3.4 compare_select_fusion
  168.1 160.6 %all-gather.5.cloned.1.call-done = bf16[8192,768]{1,0:T(8,128)(2,1)} async-done(((bf16[128,768]{1,0:T(8,128)(2,1)}), bf16[8192,768]{1,0:T(8,128)(2,1)}) %all-gather.5.cloned.1.call-update) | async-done | bytes 12582928 | tf_op jit(solution)/shard_map/all_gather | solution.py:68
  328.8 9.3 %fusion.4 = bf16[256,768]{1,0:T(8,128)(2,1)S(1)} fusion(bf16[256,8192]{1,0:T(8,128)(2,1)} %all-gather.7.cloned.1.call-done, bf16[8192,768]{1,0:T(8,128)(2,1)} %all-gather.5.cloned.1.call-done), kind=kOutput, calls=%fused_computation.10 | convolution fusion | flops 3221422080 | bytes 17170432 | tf_op jit(solution)/shard_map/dot_general | solution.py:66
  338.0 1.3 collective-permute-start
  339.4 1.7 collective-permute-done
  341.2 0.5 multiply_convert_fusion.1
  341.7 0.3 reshape.104
  342.0 0.3 copy.42
  342.4 0.3 fusion.15
  342.6 0.8 slice_add_fusion
  343.6 23.8 %all-gather = f32[32,1,8]{2,1,0:T(1,128)S(1)} all-gather(f32[1,1,8]{2,1,0:T(1,128)S(1)} %get-tuple-element.87), channel_id=1, replica_groups=mesh['fsdp'=2,'seq'=32,'tp'=8] {'seq'}, dimensions={0}, use_global_device_ids=true | all-gather | bytes 1056 | tf_op jit(solution)/shard_map/all_gather | solution.py:20
  367.6 37.6 %all-gather.9.cloned.1.call-done = f32[32,8,128,64]{2,3,1,0:T(8,128)} async-done(((f32[1,8,128,64]{2,3,1,0:T(8,128)}), f32[32,8,128,64]{2,3,1,0:T(8,128)}) %all-gather.9.cloned.1.call-update) | async-done | bytes 8388624 | tf_op jit(solution)/shard_map/all_gather | solution.py:20
  405.2 42.7 %while.12 = (s32[]{:T(128)}, f32[8,128,64]{2,1,0:T(8,128)S(1)}, s32[]{:T(128)}, f32[32,8]{1,0:T(8,128)S(1)}, f32[32,8,128,64]{2,3,1,0:T(8,128)}, /*index=5*/s32[]{:T(128)}, s32[]{:T(128)}, s32[]{:T(128)}) while((s32[]{:T(128)}, f32[8,128,64]{2,1,0:T(8,128)S(1)}, s32[]{:T(128)}, f32[32,8]{1,0:T(8,128)S(1)}, f32[32,8,128,64]{2,3,1,0:T(8,128)}, ...), condition=%wide.region_2.3_spmd, body=%wide.region_1.2_spmd.sunk | while | flops 131077 | bytes 1835231 | solution.py:28
  405.2 1.0 constant_dynamic-slice_fusion.2
  406.2 0.2 copy.63
  406.6 1.0 constant_dynamic-slice_fusion.2
  407.6 0.2 copy.63
  408.0 1.0 constant_dynamic-slice_fusion.2
  409.4 1.0 constant_dynamic-slice_fusion.2
  410.7 1.0 constant_dynamic-slice_fusion.2
  412.1 1.0 constant_dynamic-slice_fusion.2
  413.5 1.0 constant_dynamic-slice_fusion.2
  414.9 1.0 constant_dynamic-slice_fusion.2
  416.2 1.0 constant_dynamic-slice_fusion.2
  417.2 0.2 copy.63
  417.6 1.0 constant_dynamic-slice_fusion.2
  418.6 0.2 copy.63
  419.0 1.0 constant_dynamic-slice_fusion.2
  420.0 0.2 copy.63
  420.4 1.0 constant_dynamic-slice_fusion.2
  421.7 1.0 constant_dynamic-slice_fusion.2
  423.1 1.0 constant_dynamic-slice_fusion.2
  424.5 1.0 constant_dynamic-slice_fusion.2
  425.9 1.0 constant_dynamic-slice_fusion.2
  427.3 1.0 constant_dynamic-slice_fusion.2
  428.6 1.0 constant_dynamic-slice_fusion.2
  430.0 1.0 constant_dynamic-slice_fusion.2
  431.0 0.2 copy.63
  431.4 1.0 constant_dynamic-slice_fusion.2
  432.4 0.2 copy.63
  432.8 1.0 constant_dynamic-slice_fusion.2
  433.7 0.2 copy.63
  434.1 1.0 constant_dynamic-slice_fusion.2
  435.5 1.0 constant_dynamic-slice_fusion.2
  436.9 1.0 constant_dynamic-slice_fusion.2
  438.3 1.0 constant_dynamic-slice_fusion.2
  439.6 1.0 constant_dynamic-slice_fusion.2
  441.0 1.0 constant_dynamic-slice_fusion.2
  442.4 1.0 constant_dynamic-slice_fusion.2
  443.8 1.0 constant_dynamic-slice_fusion.2
  445.1 1.0 constant_dynamic-slice_fusion.2
  446.5 1.0 constant_dynamic-slice_fusion.2
  448.2 0.4 fusion.2
  448.6 0.6 fusion.3
  449.2 0.3 copy.52
  449.6 1.0 reshape.103
  (116 shorter events, 10.8 us)
Async XLA Ops:
  6.5 161.3 %copy-start = (f32[8]{0:T(128)S(1)}, f32[8]{0:T(128)}, u32[]{:S(2)}) copy-start(f32[8]{0:T(128)} %param.22) | copy-start | bytes 100
  6.5 157.7 %all-gather.7.cloned.1.call-start = ((), (), s32[]{:S(2)}) async-start(), calls=%async_computation.1 | async-start | bytes 4718592 | tf_op jit(solution)/shard_map/all_gather | solution.py:61
  7.3 321.5 %all-gather.5.cloned.1.call-start = ((), (), s32[]{:S(2)}) async-start(), calls=%async_computation | async-start | bytes 12779520 | tf_op jit(solution)/shard_map/all_gather | solution.py:68
  14.5 390.6 %all-gather.9.cloned.1.call-start = ((), (), s32[]{:S(2)}) async-start(), calls=%async_computation.2 | async-start | bytes 8650752 | tf_op jit(solution)/shard_map/all_gather | solution.py:20
  338.0 3.1 collective-permute-start
  405.2 43.5 %copy-start.1 = (f32[8]{0:T(128)S(1)}, f32[8]{0:T(128)}, u32[]{:S(2)}) copy-start(f32[8]{0:T(128)} %param.23) | copy-start | bytes 100
Sparse Core Ops, SparseCore 0:
  9.4 109.3 all-gather.6
  123.3 205.4 all-gather.4
  343.6 61.5 all-gather.8
where the time goes:
time: 458 us; the launch traced here: 457 us
  waiting for transfers between devices  201 us (44%)
  blocking collectives  172 us (38%)
  local copies, waits for them, and re-layouts  42.2 us (9%)
  between operations  15.8 us (3%)
  matrix products  14.1 us (3%)
  other arithmetic  9.38 us (2%)
    all_gather x1, waiting for transfers between devices, body(): lax.all_gather(weight_all, ('fsdp', 'seq'), axis=0, tiled=True)  161 us
    all_gather x1, blocking collectives, body(): lax.all_gather(dt_weight, ('fsdp', 'seq'), axis=0, tiled=True)  148 us
    all_gather x1, waiting for transfers between devices, prefix(): gathered = jax.tree.map(lambda a: lax.all_gather(a, axis), part)  37.6 us
    dynamic_slice x62, local copies, waits for them, and re-layouts, one(): lax.dynamic_index_in_dim(a, hop, 0, False)  36.4 us
    all_gather x1, blocking collectives, prefix(): gathered = jax.tree.map(lambda a: lax.all_gather(a, axis), part)  23.8 us
    dot_general x1, matrix products, body(): jnp.dot(rows_all, lax.all_gather(weight_all, ('fsdp', 'seq'), axis=0, til...  9.25 us
  transfers between devices with their start and end apart: 4, of which 3 were waited for; matrix products, arithmetic and copies ran while one was open for 2% of the time, Pallas kernels for 0%

commit v1 on v0

--- a/solution.py
+++ b/solution.py
@@ -1,31 +1,17 @@
 import jax
 import jax.numpy as jnp
 from jax import lax
+from jax.experimental import pallas as pl
+from jax.experimental.pallas import tpu as pltpu
 from jax.sharding import PartitionSpec as P
 
 P_SIZE = 64
 N = 128
 CONV = 4
 SPAN = 128
-
-
-def shifted(shard, axis, by):
-    count = lax.axis_size(axis)
-    pairs = [(i, i + by) for i in range(count) if 0 <= i + by < count]
-    return lax.ppermute(shard, axis, pairs)
-
-
-def prefix(part, axis, combine, identity):
-    place = lax.axis_index(axis)
-    gathered = jax.tree.map(lambda a: lax.all_gather(a, axis), part)
-    state = jax.tree.map(lambda a, e: jnp.zeros_like(a) + jnp.asarray(e, a.dtype), part, identity)
-
-    def one(hop, state):
-        return combine(
-            state, jax.tree.map(lambda a: lax.dynamic_index_in_dim(a, hop, 0, False), gathered)
-        )
-
-    return lax.fori_loop(0, place, one, state)
+MESH = pl.DeviceIdType.MESH
+WIDTH = 896
+ROWS = 32
 
 
 def sampled(mean_part, dev_part, swag_coef):
@@ -34,6 +20,263 @@
     for member in range(dev_part.shape[0]):
         accum = accum + factor * swag_coef[member] * dev_part[member].astype(jnp.float32)
     return accum.astype(jnp.bfloat16)
+
+
+def project_kernel(
+    tok_ref, w_ref, out_ref, dt_ref,
+    x_buf, w_buf, stage, relay, part, other,
+    tok_send, tok_recv, pair_send, pair_recv, w_send, w_recv, fx_send, fx_recv, ex_send, ex_recv, own_sem,
+):
+    f = lax.axis_index("fsdp")
+    s = lax.axis_index("seq")
+    t = lax.axis_index("tp")
+    core = lax.rem(s, 2)
+    y = lax.rem(lax.div(s, 2), 4)
+    x = lax.div(s, 8)
+
+    def wrap(value):
+        return lax.rem(value + 4, 4)
+
+    def place(x_at, y_at, core_at):
+        return (f, x_at * 8 + y_at * 2 + core_at, t)
+
+    sibling = place(x, y, 1 - core)
+    nexts = {"y": place(x, wrap(y + 1), core), "x": place(wrap(x + 1), y, core)}
+    prevs = {"y": place(x, wrap(y - 1), core), "x": place(wrap(x - 1), y, core)}
+    z_next, z_prev = (f, s, lax.min(t + 1, 7)), (f, s, lax.max(t - 1, 0))
+    z = f * 8 + t
+    up, down = lax.rem(z + 4, 16), lax.rem(z + 12, 16)
+    f_up, f_down = lax.div(up, 8), lax.div(down, 8)
+    z_up, z_down = (f_up, s, lax.rem(up, 8)), (f_down, s, lax.rem(down, 8))
+
+    own = pltpu.make_async_copy(w_ref, w_buf.at[f, x, y], own_sem)
+    own.start()
+    barrier = pltpu.get_barrier_semaphore()
+    for peer in (sibling, nexts["y"], prevs["y"], nexts["x"], prevs["x"], z_up, z_down):
+        pl.semaphore_signal(barrier, inc=1, device_id=peer, device_id_type=MESH)
+
+    @pl.when(t < 7)
+    def _():
+        pl.semaphore_signal(barrier, inc=1, device_id=z_next, device_id_type=MESH)
+
+    @pl.when(t > 0)
+    def _():
+        pl.semaphore_signal(barrier, inc=1, device_id=z_prev, device_id_type=MESH)
+
+    for mine in range(2):
+
+        @pl.when(core == mine)
+        def _():
+            for j in range(32):
+                here = slice(j * 128, (j + 1) * 128)
+                keep, give = 2 * j + mine, 2 * j + 1 - mine
+                x_buf[t, mine * ROWS:(mine + 1) * ROWS, here] = tok_ref[:, keep * 128:(keep + 1) * 128]
+                stage[:, here] = tok_ref[:, give * 128:(give + 1) * 128]
+
+    @pl.when((t > 0) & (t < 7))
+    def _():
+        pl.semaphore_wait(barrier, 9)
+
+    @pl.when((t == 0) | (t == 7))
+    def _():
+        pl.semaphore_wait(barrier, 8)
+
+    rows = [pl.ds(core * ROWS, ROWS), pl.ds((1 - core) * ROWS, ROWS)]
+    sends = []
+
+    def remote(src, dst, send_sem, recv_sem, peer):
+        return pltpu.make_async_remote_copy(
+            src_ref=src, dst_ref=dst, send_sem=send_sem, recv_sem=recv_sem,
+            device_id=peer, device_id_type=MESH,
+        )
+
+    def launch(copy, condition=None):
+        if condition is None:
+            copy.start()
+        else:
+            pl.when(condition)(copy.start)
+        sends.append((copy, condition))
+
+    def token_send(k, b):
+        for way, (unit, peer, condition) in enumerate((
+            (lax.max(t - k, 0), z_next, (t < 7) & (t >= k)),
+            (lax.min(t + k, 7), z_prev, (t > 0) & (t + k <= 7)),
+        )):
+            piece = x_buf.at[unit, rows[b]]
+            launch(remote(piece, piece, tok_send.at[way, k, b], tok_recv.at[way, k, b], peer), condition)
+
+    def token_wait(k, b):
+        for way, (unit, condition) in enumerate((
+            (lax.max(t - 1 - k, 0), t - 1 >= k),
+            (lax.min(t + 1 + k, 7), t + 1 + k <= 7),
+        )):
+            piece = x_buf.at[unit, rows[b]]
+
+            @pl.when(condition)
+            def _():
+                remote(piece, piece, tok_send.at[way, k, b], tok_recv.at[way, k, b], z_next).wait_recv()
+
+    def token_step(k, b):
+        token_wait(k, b)
+        token_send(k + 1, b)
+
+    halves = (pl.ds(0, 64), pl.ds(64, 64))
+    lines = (y, wrap(y - 1), wrap(y + 1), wrap(y + 2))
+
+    def block(g, phase, shift):
+        source = f if g == 0 else 1 - f
+        if phase == 0:
+            return w_buf.at[source, x, wrap(y + shift)]
+        return w_buf.at[source, wrap(x + shift), lines[phase - 1]]
+
+    def axis(phase):
+        return "y" if phase == 0 else "x"
+
+    def w_copy(g, phase, kind, piece):
+        peer = (nexts if kind % 2 == 0 else prevs)[axis(phase)]
+        return remote(piece, piece, w_send.at[g, phase, kind], w_recv.at[g, phase, kind], peer)
+
+    def w_start(g, phase):
+        for kind in range(2):
+            launch(w_copy(g, phase, kind, block(g, phase, 0)))
+
+    def w_forward(g, phase):
+        for kind, shift in ((0, -1), (1, 1)):
+            w_copy(g, phase, kind, block(g, phase, shift)).wait_recv()
+            launch(w_copy(g, phase, 2 + kind, block(g, phase, shift).at[halves[kind]]))
+
+    def w_finish(g, phase):
+        for kind in range(2):
+            w_copy(g, phase, 2 + kind, block(g, phase, 2).at[halves[kind]]).wait_recv()
+
+    pair = remote(stage, x_buf.at[t, rows[0]], pair_send, pair_recv, sibling)
+    launch(pair)
+    token_send(0, 0)
+    own.wait()
+    w_start(0, 0)
+    w_start(0, 1)
+    for kind, peer in ((0, z_up), (1, z_down)):
+        launch(remote(w_buf.at[f, x, y, halves[kind]], relay.at[kind], fx_send.at[0, kind], fx_recv.at[0, kind], peer))
+    remote(stage, x_buf.at[t, rows[1]], pair_send, pair_recv, sibling).wait_recv()
+    token_send(0, 1)
+
+    w_forward(0, 0)
+    w_start(0, 2)
+    token_step(0, 0)
+    w_forward(0, 1)
+    w_start(0, 3)
+    for kind, (peer, source) in enumerate(((z_up, f_down), (z_down, f_up))):
+        remote(relay.at[kind], relay.at[kind], fx_send.at[0, kind], fx_recv.at[0, kind], peer).wait_recv()
+        launch(remote(relay.at[kind], w_buf.at[source, x, y, halves[kind]], fx_send.at[1, kind], fx_recv.at[1, kind], peer))
+    w_finish(0, 0)
+    w_start(0, 4)
+    token_step(0, 1)
+    w_forward(0, 2)
+    token_step(1, 0)
+    for kind, peer in ((0, z_up), (1, z_down)):
+        there = w_buf.at[1 - f, x, y, halves[kind]]
+        remote(relay.at[kind], there, fx_send.at[1, kind], fx_recv.at[1, kind], peer).wait_recv()
+    w_start(1, 0)
+    w_start(1, 1)
+    w_forward(0, 3)
+    token_step(1, 1)
+    w_forward(1, 0)
+    w_start(1, 2)
+    w_forward(0, 4)
+    token_step(2, 0)
+    w_start(1, 3)
+    w_finish(1, 0)
+    w_start(1, 4)
+    token_step(2, 1)
+    w_forward(1, 1)
+    token_step(3, 0)
+    w_forward(1, 2)
+    token_step(3, 1)
+    token_step(4, 0)
+    w_forward(1, 3)
+    token_step(4, 1)
+    w_forward(1, 4)
+    token_step(5, 0)
+    token_step(5, 1)
+    for g in range(2):
+        for phase in range(1, 5):
+            w_finish(g, phase)
+
+    def multiply(first, count, kind):
+        for start in range(0, WIDTH, 256):
+            stop = min(start + 256, WIDTH)
+            weight = w_buf[:, :, :, :, start:stop].reshape(4096, stop - start)
+            units = x_buf[pl.ds(first, count)].reshape(count * 64, 4096)
+            product = jnp.dot(units, weight, preferred_element_type=jnp.float32)
+            part[pl.ds(first, count), :, :, start:stop] = product.reshape(count, 2, ROWS, stop - start)
+        swap = remote(
+            part.at[pl.ds(first, count), 1 - core], other.at[pl.ds(first, count)],
+            ex_send.at[kind], ex_recv.at[kind], sibling,
+        )
+        launch(swap)
+        return swap
+
+    low = t < 4
+    near = multiply(jnp.where(low, 0, 2), 6, 0)
+    token_wait(6, 0)
+    token_wait(6, 1)
+    far = multiply(jnp.where(low, 6, 0), 2, 1)
+    near.wait_recv()
+    far.wait_recv()
+    total = part[:, core] + other[...]
+    out_ref[...] = total[:, :, :768].reshape(8 * ROWS, 768).astype(jnp.bfloat16)
+    dt_ref[...] = total[:, :, 768:].reshape(8 * ROWS, WIDTH - 768)
+    for copy, condition in sends:
+        if condition is None:
+            copy.wait_send()
+        else:
+            pl.when(condition)(copy.wait_send)
+
+
+def project(tokens, weight):
+    vmem = pl.BlockSpec(memory_space=pltpu.VMEM)
+    dma = pltpu.SemaphoreType.DMA
+    return pl.pallas_call(
+        project_kernel,
+        out_shape=(
+            jax.ShapeDtypeStruct((256, 768), jnp.bfloat16),
+            jax.ShapeDtypeStruct((256, WIDTH - 768), jnp.float32),
+        ),
+        in_specs=[vmem, vmem],
+        out_specs=(vmem, vmem),
+        scratch_shapes=[
+            pltpu.VMEM((8, 2 * ROWS, 4096), jnp.bfloat16),
+            pltpu.VMEM((2, 4, 4, 128, WIDTH), jnp.bfloat16),
+            pltpu.VMEM((ROWS, 4096), jnp.bfloat16),
+            pltpu.VMEM((2, 64, WIDTH), jnp.bfloat16),
+            pltpu.VMEM((8, 2, ROWS, WIDTH), jnp.float32),
+            pltpu.VMEM((8, ROWS, WIDTH), jnp.float32),
+            dma((2, 7, 2)), dma((2, 7, 2)), dma(()), dma(()),
+            dma((2, 5, 4)), dma((2, 5, 4)), dma((2, 2)), dma((2, 2)), dma((2,)), dma((2,)), dma(()),
+        ],
+        compiler_params=pltpu.CompilerParams(
+            collective_id=0, has_side_effects=True, vmem_limit_bytes=56 * 2**20
+        ),
+        name="project",
+    )(tokens, weight)
+
+def shifted(shard, axis, by):
+    count = lax.axis_size(axis)
+    pairs = [(i, i + by) for i in range(count) if 0 <= i + by < count]
+    return lax.ppermute(shard, axis, pairs)
+
+
+def prefix(part, axis, combine, identity):
+    place = lax.axis_index(axis)
+    gathered = jax.tree.map(lambda a: lax.all_gather(a, axis), part)
+    state = jax.tree.map(lambda a, e: jnp.zeros_like(a) + jnp.asarray(e, a.dtype), part, identity)
+
+    def one(hop, state):
+        return combine(
+            state, jax.tree.map(lambda a: lax.dynamic_index_in_dim(a, hop, 0, False), gathered)
+        )
+
+    return lax.fori_loop(0, place, one, state)
 
 
 def combine(former, latter):
@@ -58,24 +301,13 @@
     groups_here = bc_mean.shape[2] // N
     width_x = proj_mean.shape[1]
     width_bc = 2 * bc_mean.shape[2]
-    rows_all = lax.all_gather(tokens, "tp", axis=0, tiled=True)
-    tok_count = rows_all.shape[0]
+    tok_count = 256
     weight_x = sampled(proj_mean, proj_devs, swag_coef)
     weight_bc = sampled(bc_mean, bc_devs, swag_coef).reshape(bc_mean.shape[0], width_bc)
-    weight_all = jnp.concatenate([weight_x, weight_bc], axis=1)
-    projected = jnp.dot(
-        rows_all,
-        lax.all_gather(weight_all, ("fsdp", "seq"), axis=0, tiled=True),
-        preferred_element_type=jnp.float32,
-    ).astype(jnp.bfloat16)
-    step_size = jax.nn.softplus(
-        jnp.dot(
-            rows_all,
-            lax.all_gather(dt_weight, ("fsdp", "seq"), axis=0, tiled=True),
-            preferred_element_type=jnp.float32,
-        )
-        + dt_bias
-    )
+    padding = jnp.zeros((bc_mean.shape[0], WIDTH - width_x - width_bc - heads_here), jnp.bfloat16)
+    weight_all = jnp.concatenate([weight_x, weight_bc, dt_weight, padding], axis=1)
+    projected, logits = project(tokens, weight_all)
+    step_size = jax.nn.softplus(logits[:, :heads_here] + dt_bias)
     rim_rows = shifted(projected[tok_count - (CONV - 1) :], "seq", 1)
     padded = jnp.concatenate([rim_rows, projected], axis=0).astype(jnp.float32)
     kernel = jnp.concatenate([conv_proj, conv_bc.reshape(CONV, width_bc)], axis=1)
@@ -89,7 +321,10 @@
     keys_b = conved[:, width_x : width_x + width_bc // 2].reshape(blocks, SPAN, groups_here, N)
     reads_c = conved[:, width_x + width_bc // 2 :].reshape(blocks, SPAN, groups_here, N)
     steps_b = step_size.reshape(blocks, SPAN, heads_here)
-    cum_log = jnp.cumsum(-steps_b * decay_rate, axis=1)
+    cum_log = jnp.einsum(
+        "ts,bsh->bth", jnp.tril(jnp.ones((SPAN, SPAN), jnp.float32)), -steps_b * decay_rate,
+        precision=lax.Precision.HIGHEST,
+    )
     last_cum = cum_log[:, SPAN - 1 :, :]
     scaled = (
         values.astype(jnp.float32) * (jnp.exp(last_cum - cum_log) * steps_b)[..., None]

time: 458 us -> 259 us (0.57)
  waiting for transfers between devices: 201 us -> 43.8 us
  blocking collectives: 172 us -> 19.5 us
  Pallas kernels: 0 us -> 118 us
  matrix products: 14.1 us -> 2.33 us
    all_gather x2 -> x0, waiting for transfers between devices: 161 us -> none  [the longest x1 161 us: body(): lax.all_gather(weight_all, ('fsdp', 'seq'), axis=0, tiled=True)]
    all_gather x1 -> x0, blocking collectives: 148 us -> none  [body(): lax.all_gather(dt_weight, ('fsdp', 'seq'), axis=0, tiled=True)]
    pallas_call x0 -> x1, Pallas kernels: none -> 118 us  [project(): pl.pallas_call(project_kernel, out_shape=(jax.ShapeDtypeStruct((256, 768)...]
    dot_general x2 -> x1, matrix products: 12.6 us -> 0.88 us  [body(): jnp.einsum('ts,bsh->bth', jnp.tril(jnp.ones((SPAN, SPAN), jnp.float32)),...]
    all_gather x1, waiting for transfers between devices: 37.6 us -> 43.7 us  [prefix(): gathered = jax.tree.map(lambda a: lax.all_gather(a, axis), part)]
  transfers between devices with their start and end apart: 4 -> 2, of which waited for: 3 -> 1; matrix products, arithmetic and copies ran while one was open for 2% -> 2% of each run, Pallas kernels for 0% -> 0%
where the time goes in v1:
time: 259 us; the launch traced here: 257 us
  Pallas kernels  118 us (46%)
  local copies, waits for them, and re-layouts  43.8 us (17%)
  waiting for transfers between devices  43.8 us (17%)
  blocking collectives  19.5 us (8%)
  between operations  16.2 us (6%)
  other arithmetic  11.2 us (4%)
    pallas_call x1, Pallas kernels, project(): pl.pallas_call(project_kernel, out_shape=(jax.ShapeDtypeStruct((256, 768)...  118 us
    all_gather x1, waiting for transfers between devices, prefix(): gathered = jax.tree.map(lambda a: lax.all_gather(a, axis), part)  43.7 us
    dynamic_slice x62, local copies, waits for them, and re-layouts, one(): lax.dynamic_index_in_dim(a, hop, 0, False)  36.4 us
    all_gather x1, blocking collectives, prefix(): gathered = jax.tree.map(lambda a: lax.all_gather(a, axis), part)  19.5 us
    add x32, other arithmetic, combine(): latter[0][:, None, None] * former[1] + latter[1]  5.24 us
  transfers between devices with their start and end apart: 2, of which 1 were waited for; matrix products, arithmetic and copies ran while one was open for 2% of the time, Pallas kernels for 0%

profile of v1, /device:TPU:31, one launch (start us, length us, event | category | flops | bytes accessed | tf_op | source)
XLA Modules:
  0.0 257.3 jit_solution(13474186691712466699)
XLA Ops:
  6.5 1.5 fusion.39
  10.6 0.8 copy.46
  11.4 1.2 fusion.25
  12.7 1.3 fusion.20
  14.0 0.7 maximum_maximum_fusion.w_ref
  14.8 117.9 %project.1 = (bf16[256,768]{1,0:T(8,128)(2,1)}, f32[256,128]{1,0:T(8,128)}) custom-call(bf16[32,8192]{1,0:T(8,128)(2,1)} %tok_ref.1, bf16[128,896]{1,0:T(8,128)(2,1)} %maximum_maximum_fusion.w_ref), custom_call_target="tpu_custom_call" | custom-call | tf_op jit(solution)/shard_map/project/pallas_call | solution.py:239
  132.6 0.7 slice.109
  133.3 1.3 collective-permute-start
  134.6 1.0 compare_select_fusion
  135.7 0.9 fusion.26
  136.8 0.7 constant_dynamic-update-slice_fusion.1
  137.6 0.7 constant_dynamic-update-slice_fusion
  138.3 1.1 maximum_convert_fusion
  139.4 0.5 multiply_convert_fusion.1
  139.9 0.3 reshape.95
  140.2 0.3 copy.51
  140.6 0.3 fusion.14
  140.8 0.8 slice_add_fusion
  141.7 19.5 %all-gather = f32[32,1,8]{2,1,0:T(1,128)S(1)} all-gather(f32[1,1,8]{2,1,0:T(1,128)S(1)} %get-tuple-element.96), channel_id=1, replica_groups=mesh['fsdp'=2,'seq'=32,'tp'=8] {'seq'}, dimensions={0}, use_global_device_ids=true | all-gather | bytes 1056 | tf_op jit(solution)/shard_map/all_gather | solution.py:271
  161.4 43.7 %all-gather.3.cloned.1.call-done = f32[32,8,128,64]{2,3,1,0:T(8,128)} async-done(((f32[1,8,128,64]{2,3,1,0:T(8,128)}), f32[32,8,128,64]{2,3,1,0:T(8,128)}) %all-gather.3.cloned.1.call-update) | async-done | bytes 8388624 | tf_op jit(solution)/shard_map/all_gather | solution.py:271
  205.2 42.5 %while.12 = (s32[]{:T(128)}, f32[8,128,64]{2,1,0:T(8,128)S(1)}, s32[]{:T(128)}, f32[32,8]{1,0:T(8,128)S(1)}, f32[32,8,128,64]{2,3,1,0:T(8,128)}, /*index=5*/s32[]{:T(128)}, s32[]{:T(128)}, s32[]{:T(128)}) while((s32[]{:T(128)}, f32[8,128,64]{2,1,0:T(8,128)S(1)}, s32[]{:T(128)}, f32[32,8]{1,0:T(8,128)S(1)}, f32[32,8,128,64]{2,3,1,0:T(8,128)}, ...), condition=%wide.region_1.2_spmd, body=%wide.region_0.1_spmd.sunk | while | flops 131077 | bytes 1835239 | solution.py:279
  205.3 1.0 constant_dynamic-slice_fusion.2
  206.6 1.0 constant_dynamic-slice_fusion.2
  207.6 0.2 copy.70
  208.0 1.0 constant_dynamic-slice_fusion.2
  209.4 1.0 constant_dynamic-slice_fusion.2
  210.4 0.2 copy.70
  210.7 1.0 constant_dynamic-slice_fusion.2
  212.1 1.0 constant_dynamic-slice_fusion.2
  213.5 1.0 constant_dynamic-slice_fusion.2
  214.5 0.2 copy.70
  214.9 1.0 constant_dynamic-slice_fusion.2
  216.2 1.0 constant_dynamic-slice_fusion.2
  217.6 1.0 constant_dynamic-slice_fusion.2
  218.6 0.2 copy.70
  219.0 1.0 constant_dynamic-slice_fusion.2
  220.3 1.0 constant_dynamic-slice_fusion.2
  221.7 1.0 constant_dynamic-slice_fusion.2
  223.1 1.0 constant_dynamic-slice_fusion.2
  224.5 1.0 constant_dynamic-slice_fusion.2
  225.4 0.2 copy.70
  225.8 1.0 constant_dynamic-slice_fusion.2
  227.2 1.0 constant_dynamic-slice_fusion.2
  228.6 1.0 constant_dynamic-slice_fusion.2
  229.5 0.2 copy.70
  229.9 1.0 constant_dynamic-slice_fusion.2
  231.3 1.0 constant_dynamic-slice_fusion.2
  232.7 1.0 constant_dynamic-slice_fusion.2
  233.7 0.2 copy.70
  234.1 1.0 constant_dynamic-slice_fusion.2
  235.4 1.0 constant_dynamic-slice_fusion.2
  236.4 0.2 copy.70
  236.8 1.0 constant_dynamic-slice_fusion.2
  238.2 1.0 constant_dynamic-slice_fusion.2
  239.5 1.0 constant_dynamic-slice_fusion.2
  240.9 1.0 constant_dynamic-slice_fusion.2
  242.3 1.0 constant_dynamic-slice_fusion.2
  243.6 1.0 constant_dynamic-slice_fusion.2
  245.0 1.0 constant_dynamic-slice_fusion.2
  246.4 1.0 constant_dynamic-slice_fusion.2
  248.0 0.4 fusion.2
  248.5 0.6 fusion.3
  249.1 0.3 copy.59
  249.4 1.0 reshape.94
  (107 shorter events, 10.4 us)
Async XLA Ops:
  6.5 198.6 %all-gather.3.cloned.1.call-start = ((), (), s32[]{:S(2)}) async-start(), calls=%async_computation | async-start | bytes 8650752 | tf_op jit(solution)/shard_map/all_gather | solution.py:271
  133.3 5.0 %collective-permute-start = (bf16[3,768]{1,0:T(4,128)(2,1)S(1)}, bf16[3,768]{1,0:T(4,128)(2,1)S(1)}, u32[]{:S(2)}, u32[]{:S(2)}) collective-permute-start(bf16[3,768]{1,0:T(4,128)(2,1)S(1)} %slice.109), channel_id=1, source_target_pairs={{0,8},{8,16},{16,24},{24,32},{32,40},{40,48},{48,56},{56,64},{64,7... | collective-permute-start | bytes 13832 | tf_op jit(solution)/shard_map/ppermute | solution.py:266
  205.2 43.3 %copy-start = (f32[8]{0:T(128)S(1)}, f32[8]{0:T(128)}, u32[]{:S(2)}) copy-start(f32[8]{0:T(128)} %param.23) | copy-start | bytes 100
Sparse Core Ops, SparseCore 0:
  141.8 63.3 all-gather.2

commit v2 on v1

--- a/solution.py
+++ b/solution.py
@@ -22,10 +22,26 @@
     return accum.astype(jnp.bfloat16)
 
 
-def project_kernel(
-    tok_ref, w_ref, out_ref, dt_ref,
-    x_buf, w_buf, stage, relay, part, other,
+def expand(heads):
+    lane = lax.broadcasted_iota(jnp.int32, (heads.shape[0], 128), 1)
+    return jnp.concatenate(
+        [jnp.where(lane < P_SIZE, heads[:, 2 * j:2 * j + 1], heads[:, 2 * j + 1:2 * j + 2]) for j in range(4)],
+        axis=1,
+    )
+
+
+def softplus(value):
+    small = jnp.exp(-jnp.abs(value))
+    series = small * (1.0 - small * (0.5 - small * (1.0 / 3.0 - small * 0.25)))
+    return jnp.maximum(value, 0.0) + jnp.where(small < 0.01, series, jnp.log(1.0 + small))
+
+
+def layer_kernel(
+    tok_ref, w_ref, conv_x_ref, conv_bc_ref, bias_ref, rate_ref, skip_ref, out_ref,
+    x_buf, w_buf, stage, relay, part, other, padded, edge, values, keys, reads, inner, states,
+    pair_state, pair_decay, y_state, y_decay, x_state, x_decay, give_state, give_decay, inflow, outflow, dt_buf,
     tok_send, tok_recv, pair_send, pair_recv, w_send, w_recv, fx_send, fx_recv, ex_send, ex_recv, own_sem,
+    halo_send, halo_recv, p1_send, p1_recv, p2_send, p2_recv, p4_send, p4_recv,
 ):
     f = lax.axis_index("fsdp")
     s = lax.axis_index("seq")
@@ -52,7 +68,9 @@
     own = pltpu.make_async_copy(w_ref, w_buf.at[f, x, y], own_sem)
     own.start()
     barrier = pltpu.get_barrier_semaphore()
-    for peer in (sibling, nexts["y"], prevs["y"], nexts["x"], prevs["x"], z_up, z_down):
+    y_far, x_far = place(x, wrap(y + 2), core), place(wrap(x + 2), y, core)
+    seq_next, seq_prev = (f, lax.min(s + 1, 31), t), (f, lax.max(s - 1, 0), t)
+    for peer in (sibling, nexts["y"], prevs["y"], y_far, nexts["x"], prevs["x"], x_far, z_up, z_down):
         pl.semaphore_signal(barrier, inc=1, device_id=peer, device_id_type=MESH)
 
     @pl.when(t < 7)
@@ -62,6 +80,14 @@
     @pl.when(t > 0)
     def _():
         pl.semaphore_signal(barrier, inc=1, device_id=z_prev, device_id_type=MESH)
+
+    @pl.when(s < 31)
+    def _():
+        pl.semaphore_signal(barrier, inc=1, device_id=seq_next, device_id_type=MESH)
+
+    @pl.when(s > 0)
+    def _():
+        pl.semaphore_signal(barrier, inc=1, device_id=seq_prev, device_id_type=MESH)
 
     for mine in range(2):
 
@@ -73,13 +99,8 @@
                 x_buf[t, mine * ROWS:(mine + 1) * ROWS, here] = tok_ref[:, keep * 128:(keep + 1) * 128]
                 stage[:, here] = tok_ref[:, give * 128:(give + 1) * 128]
 
-    @pl.when((t > 0) & (t < 7))
-    def _():
-        pl.semaphore_wait(barrier, 9)
-
-    @pl.when((t == 0) | (t == 7))
-    def _():
-        pl.semaphore_wait(barrier, 8)
+    ends = [t > 0, t < 7, s > 0, s < 31]
+    pl.semaphore_wait(barrier, 9 + sum(jnp.where(end, 1, 0) for end in ends))
 
     rows = [pl.ds(core * ROWS, ROWS), pl.ds((1 - core) * ROWS, ROWS)]
     sends = []
@@ -223,9 +244,157 @@
     far = multiply(jnp.where(low, 6, 0), 2, 1)
     near.wait_recv()
     far.wait_recv()
-    total = part[:, core] + other[...]
-    out_ref[...] = total[:, :, :768].reshape(8 * ROWS, 768).astype(jnp.bfloat16)
-    dt_ref[...] = total[:, :, 768:].reshape(8 * ROWS, WIDTH - 768)
+    for unit in (7, 0, 1, 2, 3, 4, 5, 6):
+        total = part[unit, core] + other[unit]
+        narrow = total[:, :768].astype(jnp.bfloat16)
+        padded[16 + unit * ROWS:16 + (unit + 1) * ROWS, :] = narrow.astype(jnp.float32)
+        dt_buf[unit * ROWS:(unit + 1) * ROWS, :] = total[:, 768:]
+        if unit == 7:
+            edge[0] = narrow[16:, :]
+            launch(remote(edge.at[0], edge.at[1], halo_send, halo_recv, seq_next), s < 31)
+
+    lane = lax.broadcasted_iota(jnp.int32, (1, 128), 1)
+
+    def row_of(ref):
+        row = jnp.zeros((1, 128), jnp.float32)
+        for head in range(8):
+            row = jnp.where(lane == head, ref[head], row)
+        return row
+
+    step = softplus(dt_buf[...] + row_of(bias_ref))
+    rise = -step * row_of(rate_ref)
+    down_to = lax.broadcasted_iota(jnp.int32, (SPAN, SPAN), 0)
+    across = lax.broadcasted_iota(jnp.int32, (SPAN, SPAN), 1)
+    causal = across <= down_to
+    triangle = jnp.where(causal, 1.0, 0.0).astype(jnp.float32)
+    steps, cums, step_rows, cum_rows, lasts = [], [], [], [], []
+    for b in range(2):
+        here = slice(b * SPAN, (b + 1) * SPAN)
+        cum = jnp.dot(
+            triangle, rise[here], precision=lax.Precision.HIGHEST, preferred_element_type=jnp.float32
+        )
+        steps.append(step[here])
+        cums.append(cum)
+        step_rows.append(step[here].T)
+        cum_rows.append(cum.T)
+        lasts.append(cum[SPAN - 1:, :])
+
+    @pl.when(s > 0)
+    def _():
+        remote(edge.at[0], edge.at[1], halo_send, halo_recv, seq_next).wait_recv()
+        padded[:16, :] = edge[1].astype(jnp.float32)
+
+    @pl.when(s == 0)
+    def _():
+        padded[:16, :] = jnp.zeros((16, 768), jnp.float32)
+
+    for tile in range(6):
+        columns = slice(tile * 128, (tile + 1) * 128)
+        gained = None
+        for tap in range(CONV):
+            if tile < 4:
+                gain = conv_x_ref[tap:tap + 1, columns]
+            else:
+                gain = conv_bc_ref[tap, tile - 4:tile - 3, :]
+            term = gain * padded[13 + tap:13 + tap + 256, columns]
+            gained = term if gained is None else gained + term
+        smooth = (gained * (1.0 / (1.0 + jnp.exp(-gained)))).astype(jnp.bfloat16)
+        if tile < 4:
+            values[:, columns] = smooth
+        elif tile == 4:
+            keys[...] = smooth
+        else:
+            reads[...] = smooth
+
+    for b in range(2):
+        here = slice(b * SPAN, (b + 1) * SPAN)
+        factor = expand(jnp.exp(lasts[b] - cums[b]) * steps[b])
+        scaled = (values[here, :].astype(jnp.float32) * factor).astype(jnp.bfloat16)
+        states[b] = lax.dot_general(
+            keys[here, :], scaled, (((0,), (0,)), ((), ())), preferred_element_type=jnp.float32
+        )
+    fades = [expand(jnp.exp(last)) for last in lasts]
+    range_state = fades[1] * states[0] + states[1]
+    range_decay = jnp.broadcast_to(fades[0] * fades[1], (8, 512))
+
+    for side in range(2):
+        half = slice(side * 256, (side + 1) * 256)
+        give_state[side] = range_state[:, half].astype(jnp.bfloat16)
+        give_decay[side] = range_decay[:, half]
+    launch(remote(give_state.at[1 - core], pair_state, p1_send.at[0], p1_recv.at[0], sibling))
+    launch(remote(give_decay.at[1 - core], pair_decay, p1_send.at[1], p1_recv.at[1], sibling))
+
+    def inside(b):
+        here = slice(b * SPAN, (b + 1) * SPAN)
+        scores = lax.dot_general(
+            reads[here, :], keys[here, :], (((1,), (1,)), ((), ())), preferred_element_type=jnp.float32
+        )
+        masked = jnp.where(causal, scores, 0.0)
+        for pair_at in range(4):
+            both = []
+            for head in (2 * pair_at, 2 * pair_at + 1):
+                gap = cums[b][:, head:head + 1] - cum_rows[b][head:head + 1, :]
+                weight = masked * jnp.exp(jnp.minimum(gap, 0.0)) * step_rows[b][head:head + 1, :]
+                both.append(jnp.dot(
+                    weight.astype(jnp.bfloat16), values[here, head * P_SIZE:(head + 1) * P_SIZE],
+                    preferred_element_type=jnp.float32,
+                ))
+            inner[here, pair_at * 128:(pair_at + 1) * 128] = jnp.concatenate(both, axis=1)
+
+    remote(give_state.at[1 - core], pair_state, p1_send.at[0], p1_recv.at[0], sibling).wait_recv()
+    remote(give_decay.at[1 - core], pair_decay, p1_send.at[1], p1_recv.at[1], sibling).wait_recv()
+    first = core == 0
+    near_state, near_decay = give_state[core].astype(jnp.float32), give_decay[core][:1]
+    far_state, far_decay = pair_state[...].astype(jnp.float32), pair_decay[:1]
+    state_0, decay_0 = jnp.where(first, near_state, far_state), jnp.where(first, near_decay, far_decay)
+    state_1, decay_1 = jnp.where(first, far_state, near_state), jnp.where(first, far_decay, near_decay)
+
+    def level(which, slots, decays, mine, state, decay, peers):
+        slots[mine] = state.astype(jnp.bfloat16)
+        decays[mine] = jnp.broadcast_to(decay, (8, 256))
+        for shift, peer in enumerate(peers):
+            launch(remote(slots.at[mine], slots.at[mine], p2_send.at[which, 0, shift], p2_recv.at[which, 0, shift], peer))
+            launch(remote(decays.at[mine], decays.at[mine], p2_send.at[which, 1, shift], p2_recv.at[which, 1, shift], peer))
+
+    def gather(which, slots, decays, mine, peers):
+        for shift, peer in enumerate(peers):
+            there = wrap(mine - 1 - shift)
+            remote(slots.at[there], slots.at[there], p2_send.at[which, 0, shift], p2_recv.at[which, 0, shift], peer).wait_recv()
+            remote(decays.at[there], decays.at[there], p2_send.at[which, 1, shift], p2_recv.at[which, 1, shift], peer).wait_recv()
+        state, decay = jnp.zeros((N, 256), jnp.float32), jnp.ones((1, 256), jnp.float32)
+        before, before_decay = state, decay
+        for member in range(4):
+            before = jnp.where(mine == member, state, before)
+            before_decay = jnp.where(mine == member, decay, before_decay)
+            fade = decays[member][:1]
+            state = fade * state + slots[member].astype(jnp.float32)
+            decay = decay * fade
+        return before, before_decay, state, decay
+
+    y_peers = [nexts["y"], y_far, prevs["y"]]
+    x_peers = [nexts["x"], x_far, prevs["x"]]
+    level(0, y_state, y_decay, y, decay_1 * state_0 + state_1, decay_0 * decay_1, y_peers)
+    inside(0)
+    before_y, before_y_decay, row_state, row_decay = gather(0, y_state, y_decay, y, y_peers)
+    level(1, x_state, x_decay, x, row_state, row_decay, x_peers)
+    inside(1)
+    before_x, _, _, _ = gather(1, x_state, x_decay, x, x_peers)
+    into_0 = before_y_decay * before_x + before_y
+    into_1 = decay_0 * into_0 + state_0
+    outflow[...] = jnp.where(first, into_1, into_0).astype(jnp.bfloat16)
+    launch(remote(outflow, inflow.at[core], p4_send, p4_recv, sibling))
+    inflow[core] = jnp.where(first, into_0, into_1).astype(jnp.bfloat16)
+    remote(outflow, inflow.at[1 - core], p4_send, p4_recv, sibling).wait_recv()
+    entering = jnp.concatenate([inflow[0], inflow[1]], axis=1)
+    skips = expand(row_of(skip_ref))
+    for b in range(2):
+        here = slice(b * SPAN, (b + 1) * SPAN)
+        outer = jnp.dot(reads[here, :], entering, preferred_element_type=jnp.float32)
+        outer = expand(jnp.exp(cums[b])) * outer
+        result = inner[here, :] + outer + skips * values[here, :].astype(jnp.float32)
+        out_ref[here, :] = result.astype(jnp.bfloat16)
+        if b == 0:
+            entering = (fades[0] * entering.astype(jnp.float32) + states[0]).astype(jnp.bfloat16)
     for copy, condition in sends:
         if condition is None:
             copy.wait_send()
@@ -233,54 +402,50 @@
             pl.when(condition)(copy.wait_send)
 
 
-def project(tokens, weight):
+def layer(tokens, weight, conv_x, conv_bc, bias, rate, skip):
     vmem = pl.BlockSpec(memory_space=pltpu.VMEM)
+    smem = pl.BlockSpec(memory_space=pltpu.SMEM)
     dma = pltpu.SemaphoreType.DMA
+    bf16, f32 = jnp.bfloat16, jnp.float32
     return pl.pallas_call(
-        project_kernel,
-        out_shape=(
-            jax.ShapeDtypeStruct((256, 768), jnp.bfloat16),
-            jax.ShapeDtypeStruct((256, WIDTH - 768), jnp.float32),
-        ),
-        in_specs=[vmem, vmem],
-        out_specs=(vmem, vmem),
+        layer_kernel,
+        out_shape=jax.ShapeDtypeStruct((256, 512), bf16),
+        in_specs=[vmem, vmem, vmem, vmem, smem, smem, smem],
+        out_specs=vmem,
         scratch_shapes=[
-            pltpu.VMEM((8, 2 * ROWS, 4096), jnp.bfloat16),
-            pltpu.VMEM((2, 4, 4, 128, WIDTH), jnp.bfloat16),
-            pltpu.VMEM((ROWS, 4096), jnp.bfloat16),
-            pltpu.VMEM((2, 64, WIDTH), jnp.bfloat16),
-            pltpu.VMEM((8, 2, ROWS, WIDTH), jnp.float32),
-            pltpu.VMEM((8, ROWS, WIDTH), jnp.float32),
+            pltpu.VMEM((8, 2 * ROWS, 4096), bf16),
+            pltpu.VMEM((2, 4, 4, 128, WIDTH), bf16),
+            pltpu.VMEM((ROWS, 4096), bf16),
+            pltpu.VMEM((2, 64, WIDTH), bf16),
+            pltpu.VMEM((8, 2, ROWS, WIDTH), f32),
+            pltpu.VMEM((8, ROWS, WIDTH), f32),
+            pltpu.VMEM((16 + 256, 768), f32),
+            pltpu.VMEM((2, 16, 768), bf16),
+            pltpu.VMEM((256, 512), bf16),
+            pltpu.VMEM((256, N), bf16),
+            pltpu.VMEM((256, N), bf16),
+            pltpu.VMEM((256, 512), f32),
+            pltpu.VMEM((2, N, 512), f32),
+            pltpu.VMEM((N, 256), bf16),
+            pltpu.VMEM((8, 256), f32),
+            pltpu.VMEM((4, N, 256), bf16),
+            pltpu.VMEM((4, 8, 256), f32),
+            pltpu.VMEM((4, N, 256), bf16),
+            pltpu.VMEM((4, 8, 256), f32),
+            pltpu.VMEM((2, N, 256), bf16),
+            pltpu.VMEM((2, 8, 256), f32),
+            pltpu.VMEM((2, N, 256), bf16),
+            pltpu.VMEM((N, 256), bf16),
+            pltpu.VMEM((256, 128), f32),
             dma((2, 7, 2)), dma((2, 7, 2)), dma(()), dma(()),
             dma((2, 5, 4)), dma((2, 5, 4)), dma((2, 2)), dma((2, 2)), dma((2,)), dma((2,)), dma(()),
+            dma(()), dma(()), dma((2,)), dma((2,)), dma((2, 2, 3)), dma((2, 2, 3)), dma(()), dma(()),
         ],
         compiler_params=pltpu.CompilerParams(
             collective_id=0, has_side_effects=True, vmem_limit_bytes=56 * 2**20
         ),
-        name="project",
-    )(tokens, weight)
-
-def shifted(shard, axis, by):
-    count = lax.axis_size(axis)
-    pairs = [(i, i + by) for i in range(count) if 0 <= i + by < count]
-    return lax.ppermute(shard, axis, pairs)
-
-
-def prefix(part, axis, combine, identity):
-    place = lax.axis_index(axis)
-    gathered = jax.tree.map(lambda a: lax.all_gather(a, axis), part)
-    state = jax.tree.map(lambda a, e: jnp.zeros_like(a) + jnp.asarray(e, a.dtype), part, identity)
-
-    def one(hop, state):
-        return combine(
-            state, jax.tree.map(lambda a: lax.dynamic_index_in_dim(a, hop, 0, False), gathered)
-        )
-
-    return lax.fori_loop(0, place, one, state)
-
-
-def combine(former, latter):
-    return (former[0] * latter[0], latter[0][:, None, None] * former[1] + latter[1])
+        name="layer",
+    )(tokens, weight, conv_x, conv_bc, bias, rate, skip)
 
 
 def body(
@@ -297,75 +462,11 @@
     conv_proj,
     conv_bc,
 ):
-    heads_here = decay_rate.shape[0]
-    groups_here = bc_mean.shape[2] // N
-    width_x = proj_mean.shape[1]
-    width_bc = 2 * bc_mean.shape[2]
-    tok_count = 256
     weight_x = sampled(proj_mean, proj_devs, swag_coef)
-    weight_bc = sampled(bc_mean, bc_devs, swag_coef).reshape(bc_mean.shape[0], width_bc)
-    padding = jnp.zeros((bc_mean.shape[0], WIDTH - width_x - width_bc - heads_here), jnp.bfloat16)
-    weight_all = jnp.concatenate([weight_x, weight_bc, dt_weight, padding], axis=1)
-    projected, logits = project(tokens, weight_all)
-    step_size = jax.nn.softplus(logits[:, :heads_here] + dt_bias)
-    rim_rows = shifted(projected[tok_count - (CONV - 1) :], "seq", 1)
-    padded = jnp.concatenate([rim_rows, projected], axis=0).astype(jnp.float32)
-    kernel = jnp.concatenate([conv_proj, conv_bc.reshape(CONV, width_bc)], axis=1)
-    conv_sum = kernel[0] * padded[0:tok_count]
-    for offset in range(1, CONV):
-        conv_sum = conv_sum + kernel[offset] * padded[offset : offset + tok_count]
-    conved = jax.nn.silu(conv_sum).astype(jnp.bfloat16)
-    blocks = tok_count // SPAN
-    per_group = heads_here // groups_here
-    values = conved[:, :width_x].reshape(blocks, SPAN, heads_here, P_SIZE)
-    keys_b = conved[:, width_x : width_x + width_bc // 2].reshape(blocks, SPAN, groups_here, N)
-    reads_c = conved[:, width_x + width_bc // 2 :].reshape(blocks, SPAN, groups_here, N)
-    steps_b = step_size.reshape(blocks, SPAN, heads_here)
-    cum_log = jnp.einsum(
-        "ts,bsh->bth", jnp.tril(jnp.ones((SPAN, SPAN), jnp.float32)), -steps_b * decay_rate,
-        precision=lax.Precision.HIGHEST,
-    )
-    last_cum = cum_log[:, SPAN - 1 :, :]
-    scaled = (
-        values.astype(jnp.float32) * (jnp.exp(last_cum - cum_log) * steps_b)[..., None]
-    ).astype(jnp.bfloat16)
-    keys_h = jnp.repeat(keys_b, per_group, axis=2)
-    states = jnp.einsum("bshn,bshp->bhnp", keys_h, scaled, preferred_element_type=jnp.float32)
-    block_decay = jnp.exp(last_cum[:, 0, :])
-    total_decay = block_decay[0]
-    total_state = states[0]
-    member = 1
-    total_decay, total_state = combine(
-        (total_decay, total_state), (block_decay[member], states[member])
-    )
-    incoming = prefix(
-        (total_decay, total_state),
-        "seq",
-        combine,
-        (jnp.ones((heads_here,), jnp.float32), jnp.zeros((heads_here, N, P_SIZE), jnp.float32)),
-    )
-    scores = jnp.einsum("bqgn,bsgn->bgqs", reads_c, keys_b, preferred_element_type=jnp.float32)
-    scores = jnp.repeat(scores, per_group, axis=1)
-    causal_mask = jnp.tril(jnp.ones((SPAN, SPAN), bool))
-    later_cum = jnp.transpose(cum_log, (0, 2, 1))
-    cum_gaps = later_cum[:, :, :, None] - later_cum[:, :, None, :]
-    decays = jnp.where(causal_mask, jnp.exp(jnp.minimum(cum_gaps, 0.0)), 0.0)
-    weights = (scores * decays * jnp.transpose(steps_b, (0, 2, 1))[:, :, None, :]).astype(
-        jnp.bfloat16
-    )
-    inner_part = jnp.einsum("bhqs,bshp->bqhp", weights, values, preferred_element_type=jnp.float32)
-    carried = incoming[1]
-    entering = []
-    for member in range(blocks):
-        entering.append(carried)
-        carried = block_decay[member][:, None, None] * carried + states[member]
-    entering_bf = jnp.stack(entering).astype(jnp.bfloat16)
-    reads_h = jnp.repeat(reads_c, per_group, axis=2)
-    outer_part = jnp.exp(cum_log)[..., None] * jnp.einsum(
-        "bqhn,bhnp->bqhp", reads_h, entering_bf, preferred_element_type=jnp.float32
-    )
-    result = inner_part + outer_part + skip_gain[:, None] * values.astype(jnp.float32)
-    return result.reshape(tok_count, width_x).astype(jnp.bfloat16)
+    weight_bc = sampled(bc_mean, bc_devs, swag_coef).reshape(128, 256)
+    padding = jnp.zeros((128, WIDTH - 768 - 8), jnp.bfloat16)
+    weight = jnp.concatenate([weight_x, weight_bc, dt_weight, padding], axis=1)
+    return layer(tokens, weight, conv_proj, conv_bc, dt_bias, decay_rate, skip_gain)
 
 
 def solution(mesh):

time: 259 us -> 148 us (0.57)
  the two profiles are of different devices: /device:TPU:31 before, /device:TPU:1 now
where the time goes in v2:
time: 148 us
  Pallas kernels  138 us (93%)
  local copies, waits for them, and re-layouts  4.02 us (3%)
  other arithmetic  2.95 us (2%)
  between operations  2.5 us (2%)
    pallas_call x1, Pallas kernels, layer(): pl.pallas_call(layer_kernel, out_shape=jax.ShapeDtypeStruct((256, 512), b...  138 us

profile of v2, /device:TPU:1, one launch (start us, length us, event | category | flops | bytes accessed | tf_op | source)
XLA Modules:
  0.0 147.9 jit_solution(10870877965338558245)
XLA Ops:
  0.0 0.0 copy-start.1
  0.0 0.0 copy-start
  0.0 0.1 pad.3.clone
  0.1 1.4 fusion.2
  4.0 0.8 copy.13
  4.8 0.0 copy-done.1
  4.8 1.2 fusion.1
  6.0 0.0 copy-done
  6.0 1.0 fusion
  7.1 0.7 maximum_maximum_fusion.w_ref
  7.8 138.4 %layer.1 = bf16[256,512]{1,0:T(8,128)(2,1)} custom-call(bf16[32,8192]{1,0:T(8,128)(2,1)} %tok_ref.1, bf16[128,896]{1,0:T(8,128)(2,1)} %maximum_maximum_fusion.w_ref, f32[4,512]{1,0:T(4,128)} %conv_x_ref.1, f32[4,2,128]{2,1,0:T(2,128)} %conv_bc_ref.1, f32[8]{0:T(128)} %bias_ref.1, f32[8]{0:T(128)} %rate_ref.1, f32[8]{0:T(128)} %skip_ref.1), custom_call_target="tpu_custom_call" | custom-call | tf_op jit(solution)/shard_map/layer/pallas_call | solution.py:410
  146.2 1.7 %copy.18 = bf16[256,512]{1,0:T(8,128)(2,1)} copy(bf16[256,512]{1,0:T(8,128)(2,1)} %layer.1) | data formatting | bytes 524288
  (2 shorter events, 0.0 us)
Async XLA Ops:
  0.0 4.8 %copy-start.1 = (bf16[128,2,128]{2,1,0:T(2,128)(2,1)S(1)}, bf16[128,2,128]{2,1,0:T(2,128)(2,1)}, u32[]{:S(2)}) copy-start(bf16[128,2,128]{2,1,0:T(2,128)(2,1)} %param.15) | copy-start | bytes 196612
  0.0 6.0 %copy-start = (bf16[4,128,512]{2,1,0:T(8,128)(2,1)S(1)}, bf16[4,128,512]{2,1,0:T(8,128)(2,1)}, u32[]{:S(2)}) copy-start(bf16[4,128,512]{2,1,0:T(8,128)(2,1)} %param.14) | copy-start | bytes 1572868

commit v3 on v2

--- a/solution.py
+++ b/solution.py
@@ -10,7 +10,7 @@
 CONV = 4
 SPAN = 128
 MESH = pl.DeviceIdType.MESH
-WIDTH = 896
+SHARE = 112
 ROWS = 32
 
 
@@ -36,19 +36,35 @@
     return jnp.maximum(value, 0.0) + jnp.where(small < 0.01, series, jnp.log(1.0 + small))
 
 
+def fold(tile):
+    lane = lax.broadcasted_iota(jnp.int32, tile.shape, 1)
+    joined = jnp.where(lane == 96, tile + pltpu.roll(tile, 127, 1), tile)
+    return jnp.where(lane == 97, 0.0, joined)
+
+
+def pack(tile):
+    lane = lax.broadcasted_iota(jnp.int32, tile.shape, 1)
+    high = tile.astype(jnp.bfloat16).astype(jnp.float32)
+    low = pltpu.roll(tile - high, 1, 1)
+    return jnp.where(lane == 97, low, high).astype(jnp.bfloat16)
+
+
 def layer_kernel(
     tok_ref, w_ref, conv_x_ref, conv_bc_ref, bias_ref, rate_ref, skip_ref, out_ref,
-    x_buf, w_buf, stage, relay, part, other, padded, edge, values, keys, reads, inner, states,
+    x_buf, ring, rs_out, rs_own, rs_in, z_out, z_in, y_in, padded, edge, values, keys, reads, inner, states,
     pair_state, pair_decay, y_state, y_decay, x_state, x_decay, give_state, give_decay, inflow, outflow, dt_buf,
-    tok_send, tok_recv, pair_send, pair_recv, w_send, w_recv, fx_send, fx_recv, ex_send, ex_recv, own_sem,
+    own_sem, p_send, p_recv, a_send, a_recv, u_send, u_recv, c_send, c_recv, r_send, r_recv, rs_send, rs_recv,
+    z_send, z_recv, y_send, y_recv,
     halo_send, halo_recv, p1_send, p1_recv, p2_send, p2_recv, p4_send, p4_recv,
 ):
     f = lax.axis_index("fsdp")
     s = lax.axis_index("seq")
     t = lax.axis_index("tp")
+    q = lax.rem(s, 8)
+    x = lax.div(s, 8)
     core = lax.rem(s, 2)
-    y = lax.rem(lax.div(s, 2), 4)
-    x = lax.div(s, 8)
+    y = lax.div(q, 2)
+    z = f * 8 + t
 
     def wrap(value):
         return lax.rem(value + 4, 4)
@@ -56,30 +72,23 @@
     def place(x_at, y_at, core_at):
         return (f, x_at * 8 + y_at * 2 + core_at, t)
 
+    def plane(z_at):
+        z_at = lax.rem(z_at + 16, 16)
+        return (lax.div(z_at, 8), s, lax.rem(z_at, 8))
+
     sibling = place(x, y, 1 - core)
-    nexts = {"y": place(x, wrap(y + 1), core), "x": place(wrap(x + 1), y, core)}
-    prevs = {"y": place(x, wrap(y - 1), core), "x": place(wrap(x - 1), y, core)}
-    z_next, z_prev = (f, s, lax.min(t + 1, 7)), (f, s, lax.max(t - 1, 0))
-    z = f * 8 + t
-    up, down = lax.rem(z + 4, 16), lax.rem(z + 12, 16)
-    f_up, f_down = lax.div(up, 8), lax.div(down, 8)
-    z_up, z_down = (f_up, s, lax.rem(up, 8)), (f_down, s, lax.rem(down, 8))
-
-    own = pltpu.make_async_copy(w_ref, w_buf.at[f, x, y], own_sem)
-    own.start()
+    y_next, y_far, y_prev = (place(x, wrap(y + by), core) for by in (1, 2, 3))
+    x_next, x_far, x_prev = (place(wrap(x + by), y, core) for by in (1, 2, 3))
+    z_next, z_prev = plane(z + 1), plane(z - 1)
+    q_at = [lax.rem(q + 1 + i, 8) for i in range(7)]
+    q_peers = [(f, x * 8 + at, t) for at in q_at]
+    t_at = [lax.rem(t + by, 8) for by in range(8)]
+    t_peers = [(f, s, at) for at in t_at]
+    seq_next, seq_prev = (f, lax.min(s + 1, 31), t), (f, lax.max(s - 1, 0), t)
+
     barrier = pltpu.get_barrier_semaphore()
-    y_far, x_far = place(x, wrap(y + 2), core), place(wrap(x + 2), y, core)
-    seq_next, seq_prev = (f, lax.min(s + 1, 31), t), (f, lax.max(s - 1, 0), t)
-    for peer in (sibling, nexts["y"], prevs["y"], y_far, nexts["x"], prevs["x"], x_far, z_up, z_down):
+    for peer in (x_next, x_far, x_prev, z_next, z_prev, *q_peers, *t_peers[1:]):
         pl.semaphore_signal(barrier, inc=1, device_id=peer, device_id_type=MESH)
-
-    @pl.when(t < 7)
-    def _():
-        pl.semaphore_signal(barrier, inc=1, device_id=z_next, device_id_type=MESH)
-
-    @pl.when(t > 0)
-    def _():
-        pl.semaphore_signal(barrier, inc=1, device_id=z_prev, device_id_type=MESH)
 
     @pl.when(s < 31)
     def _():
@@ -89,20 +98,6 @@
     def _():
         pl.semaphore_signal(barrier, inc=1, device_id=seq_prev, device_id_type=MESH)
 
-    for mine in range(2):
-
-        @pl.when(core == mine)
-        def _():
-            for j in range(32):
-                here = slice(j * 128, (j + 1) * 128)
-                keep, give = 2 * j + mine, 2 * j + 1 - mine
-                x_buf[t, mine * ROWS:(mine + 1) * ROWS, here] = tok_ref[:, keep * 128:(keep + 1) * 128]
-                stage[:, here] = tok_ref[:, give * 128:(give + 1) * 128]
-
-    ends = [t > 0, t < 7, s > 0, s < 31]
-    pl.semaphore_wait(barrier, 9 + sum(jnp.where(end, 1, 0) for end in ends))
-
-    rows = [pl.ds(core * ROWS, ROWS), pl.ds((1 - core) * ROWS, ROWS)]
     sends = []
 
     def remote(src, dst, send_sem, recv_sem, peer):
@@ -118,142 +113,168 @@
             pl.when(condition)(copy.start)
         sends.append((copy, condition))
 
-    def token_send(k, b):
-        for way, (unit, peer, condition) in enumerate((
-            (lax.max(t - k, 0), z_next, (t < 7) & (t >= k)),
-            (lax.min(t + k, 7), z_prev, (t > 0) & (t + k <= 7)),
-        )):
-            piece = x_buf.at[unit, rows[b]]
-            launch(remote(piece, piece, tok_send.at[way, k, b], tok_recv.at[way, k, b], peer), condition)
-
-    def token_wait(k, b):
-        for way, (unit, condition) in enumerate((
-            (lax.max(t - 1 - k, 0), t - 1 >= k),
-            (lax.min(t + 1 + k, 7), t + 1 + k <= 7),
-        )):
-            piece = x_buf.at[unit, rows[b]]
-
-            @pl.when(condition)
+    def token_columns(half, x_at):
+        return tok_ref.at[:, pl.ds(pl.multiple_of(half * 4096 + x_at * 1024, 1024), 1024)]
+
+    def token_place(half, x_at, q_here):
+        return x_buf.at[x_at, q_here, :, pl.ds(half * 1024, 1024)]
+
+    locals_ = [
+        pltpu.make_async_copy(token_columns(half, x), token_place(half, x, q), own_sem.at[half]) for half in range(2)
+    ]
+    lanes = pl.ds(pl.multiple_of(q * 128, 128), 128)
+    locals_.append(pltpu.make_async_copy(w_ref.at[q], ring.at[z, :, lanes], own_sem.at[2]))
+    for copy in locals_:
+        copy.start()
+    pl.semaphore_wait(barrier, 19 + jnp.where(s > 0, 1, 0) + jnp.where(s < 31, 1, 0))
+
+    for i in range(7):
+        launch(remote(w_ref.at[q_at[i]], ring.at[z, :, lanes], p_send.at[i], p_recv.at[i], q_peers[i]))
+    for i, peer in enumerate((x_next, x_far, x_prev)):
+        for half in range(2):
+            launch(remote(
+                token_columns(half, wrap(x + 1 + i)), token_place(half, x, q), a_send.at[i, half], a_recv.at[i, half], peer
+            ))
+
+    pieces = (pl.ds(0, 48), pl.ds(48, 64))
+
+    def ring_copy(way, k, b, slot):
+        piece = ring.at[lax.rem(slot + 32, 16), pieces[b]]
+        return remote(piece, piece, r_send.at[way, k, b], r_recv.at[way, k, b], z_next if way == 0 else z_prev)
+
+    def ring_send(k, b):
+        for way in range(2):
+            if k < 7 or way == b:
+                launch(ring_copy(way, k, b, z - k if way == 0 else z + k))
+
+    def ring_wait(k, b):
+        for way in range(2):
+            if k < 7 or way == b:
+                ring_copy(way, k, b, z - 1 - k if way == 0 else z + 1 + k).wait_recv()
+
+    def ring_step(k):
+        for b in range(2):
+            ring_wait(k, b)
+            ring_send(k + 1, b)
+
+    for i in range(7):
+        from_q = pl.ds(pl.multiple_of(lax.rem(q + 7 - i, 8) * 128, 128), 128)
+        remote(w_ref.at[q_at[i]], ring.at[z, :, from_q], p_send.at[i], p_recv.at[i], q_peers[i]).wait_recv()
+    for copy in locals_:
+        copy.wait()
+    ring_send(0, 0)
+    ring_send(0, 1)
+    for i, peer in enumerate((x_next, x_far, x_prev)):
+        for half in range(2):
+            here = token_place(half, wrap(x - 1 - i), q)
+            remote(here, here, a_send.at[i, half], a_recv.at[i, half], peer).wait_recv()
+
+    def unit(y_by, core_at, part=None):
+        member = wrap(y + y_by) * 2 + core_at
+        return x_buf.at[:, member] if part is None else x_buf.at[pl.ds(2 * part, 2), member]
+
+    def unit_copy(kind, piece):
+        return remote(piece, piece, u_send.at[kind], u_recv.at[kind], y_next if kind % 2 == 0 else y_prev)
+
+    def share(index, y_by):
+        launch(remote(unit(y_by, core), unit(y_by, core), c_send.at[index], c_recv.at[index], sibling))
+
+    launch(unit_copy(0, unit(0, core)))
+    launch(unit_copy(1, unit(0, core)))
+    share(0, 0)
+    ring_step(0)
+    ring_step(1)
+    ring_step(2)
+    for kind, y_by in ((0, -1), (1, 1)):
+        unit_copy(kind, unit(y_by, core)).wait_recv()
+        launch(unit_copy(2 + kind, unit(y_by, core, kind)))
+        share(1 + kind, y_by)
+    ring_step(3)
+    for kind in range(2):
+        unit_copy(2 + kind, unit(2, core, kind)).wait_recv()
+    share(3, 2)
+    ring_step(4)
+    for index, y_by in enumerate((0, -1, 1, 2)):
+        here = unit(y_by, 1 - core)
+        remote(here, here, c_send.at[index], c_recv.at[index], sibling).wait_recv()
+
+    def multiply(by):
+        tau = t_at[by]
+        for owner in range(4):
+            total = jnp.zeros((256, SHARE), jnp.float32)
+            for half in range(2):
+                total = total + lax.dot_general(
+                    x_buf[owner, :, :, half * 1024:(half + 1) * 1024].reshape(256, 1024), ring[tau + 8 * half],
+                    (((1,), (1,)), ((), ())), preferred_element_type=jnp.float32,
+                )
+            total = jnp.concatenate([total, jnp.zeros((256, 128 - SHARE), jnp.float32)], axis=1)
+            rs_out[by, owner] = pack(total)
+
+            @pl.when(x == owner)
             def _():
-                remote(piece, piece, tok_send.at[way, k, b], tok_recv.at[way, k, b], z_next).wait_recv()
-
-    def token_step(k, b):
-        token_wait(k, b)
-        token_send(k + 1, b)
-
-    halves = (pl.ds(0, 64), pl.ds(64, 64))
-    lines = (y, wrap(y - 1), wrap(y + 1), wrap(y + 2))
-
-    def block(g, phase, shift):
-        source = f if g == 0 else 1 - f
-        if phase == 0:
-            return w_buf.at[source, x, wrap(y + shift)]
-        return w_buf.at[source, wrap(x + shift), lines[phase - 1]]
-
-    def axis(phase):
-        return "y" if phase == 0 else "x"
-
-    def w_copy(g, phase, kind, piece):
-        peer = (nexts if kind % 2 == 0 else prevs)[axis(phase)]
-        return remote(piece, piece, w_send.at[g, phase, kind], w_recv.at[g, phase, kind], peer)
-
-    def w_start(g, phase):
-        for kind in range(2):
-            launch(w_copy(g, phase, kind, block(g, phase, 0)))
-
-    def w_forward(g, phase):
-        for kind, shift in ((0, -1), (1, 1)):
-            w_copy(g, phase, kind, block(g, phase, shift)).wait_recv()
-            launch(w_copy(g, phase, 2 + kind, block(g, phase, shift).at[halves[kind]]))
-
-    def w_finish(g, phase):
-        for kind in range(2):
-            w_copy(g, phase, 2 + kind, block(g, phase, 2).at[halves[kind]]).wait_recv()
-
-    pair = remote(stage, x_buf.at[t, rows[0]], pair_send, pair_recv, sibling)
-    launch(pair)
-    token_send(0, 0)
-    own.wait()
-    w_start(0, 0)
-    w_start(0, 1)
-    for kind, peer in ((0, z_up), (1, z_down)):
-        launch(remote(w_buf.at[f, x, y, halves[kind]], relay.at[kind], fx_send.at[0, kind], fx_recv.at[0, kind], peer))
-    remote(stage, x_buf.at[t, rows[1]], pair_send, pair_recv, sibling).wait_recv()
-    token_send(0, 1)
-
-    w_forward(0, 0)
-    w_start(0, 2)
-    token_step(0, 0)
-    w_forward(0, 1)
-    w_start(0, 3)
-    for kind, (peer, source) in enumerate(((z_up, f_down), (z_down, f_up))):
-        remote(relay.at[kind], relay.at[kind], fx_send.at[0, kind], fx_recv.at[0, kind], peer).wait_recv()
-        launch(remote(relay.at[kind], w_buf.at[source, x, y, halves[kind]], fx_send.at[1, kind], fx_recv.at[1, kind], peer))
-    w_finish(0, 0)
-    w_start(0, 4)
-    token_step(0, 1)
-    w_forward(0, 2)
-    token_step(1, 0)
-    for kind, peer in ((0, z_up), (1, z_down)):
-        there = w_buf.at[1 - f, x, y, halves[kind]]
-        remote(relay.at[kind], there, fx_send.at[1, kind], fx_recv.at[1, kind], peer).wait_recv()
-    w_start(1, 0)
-    w_start(1, 1)
-    w_forward(0, 3)
-    token_step(1, 1)
-    w_forward(1, 0)
-    w_start(1, 2)
-    w_forward(0, 4)
-    token_step(2, 0)
-    w_start(1, 3)
-    w_finish(1, 0)
-    w_start(1, 4)
-    token_step(2, 1)
-    w_forward(1, 1)
-    token_step(3, 0)
-    w_forward(1, 2)
-    token_step(3, 1)
-    token_step(4, 0)
-    w_forward(1, 3)
-    token_step(4, 1)
-    w_forward(1, 4)
-    token_step(5, 0)
-    token_step(5, 1)
-    for g in range(2):
-        for phase in range(1, 5):
-            w_finish(g, phase)
-
-    def multiply(first, count, kind):
-        for start in range(0, WIDTH, 256):
-            stop = min(start + 256, WIDTH)
-            weight = w_buf[:, :, :, :, start:stop].reshape(4096, stop - start)
-            units = x_buf[pl.ds(first, count)].reshape(count * 64, 4096)
-            product = jnp.dot(units, weight, preferred_element_type=jnp.float32)
-            part[pl.ds(first, count), :, :, start:stop] = product.reshape(count, 2, ROWS, stop - start)
-        swap = remote(
-            part.at[pl.ds(first, count), 1 - core], other.at[pl.ds(first, count)],
-            ex_send.at[kind], ex_recv.at[kind], sibling,
-        )
-        launch(swap)
-        return swap
-
-    low = t < 4
-    near = multiply(jnp.where(low, 0, 2), 6, 0)
-    token_wait(6, 0)
-    token_wait(6, 1)
-    far = multiply(jnp.where(low, 6, 0), 2, 1)
-    near.wait_recv()
-    far.wait_recv()
-    for unit in (7, 0, 1, 2, 3, 4, 5, 6):
-        total = part[unit, core] + other[unit]
-        narrow = total[:, :768].astype(jnp.bfloat16)
-        padded[16 + unit * ROWS:16 + (unit + 1) * ROWS, :] = narrow.astype(jnp.float32)
-        dt_buf[unit * ROWS:(unit + 1) * ROWS, :] = total[:, 768:]
-        if unit == 7:
-            edge[0] = narrow[16:, :]
-            launch(remote(edge.at[0], edge.at[1], halo_send, halo_recv, seq_next), s < 31)
+                rs_own[by] = total
+
+        for i, peer in enumerate((x_next, x_far, x_prev)):
+            launch(remote(rs_out.at[by, wrap(x + 1 + i)], rs_in.at[by, i], rs_send.at[by, i], rs_recv.at[by, i], peer))
+
+    def settle(by):
+        total = rs_own[by]
+        for i, peer in enumerate((x_next, x_far, x_prev)):
+            remote(rs_in.at[by, i], rs_in.at[by, i], rs_send.at[by, i], rs_recv.at[by, i], peer).wait_recv()
+            total = total + rs_in[by, i].astype(jnp.float32)
+        packed = pack(fold(total))
+        if by == 0:
+            z_in[t] = packed
+        else:
+            z_out[by] = packed
+            launch(remote(z_out.at[by], z_in.at[t], z_send.at[by], z_recv.at[by], t_peers[by]))
+
+    multiply(4)
+    ring_step(5)
+    multiply(3)
+    multiply(5)
+    settle(4)
+    ring_step(6)
+    multiply(2)
+    multiply(6)
+    settle(3)
+    settle(5)
+    multiply(1)
+    multiply(7)
+    settle(2)
+    settle(6)
+    ring_wait(7, 0)
+    ring_wait(7, 1)
+    multiply(0)
+    settle(1)
+    settle(7)
+    settle(0)
+    for by in range(1, 8):
+        here = z_in.at[lax.rem(t + 8 - by, 8)]
+        remote(here, here, z_send.at[by], z_recv.at[by], t_peers[by]).wait_recv()
+    mine = pltpu.make_async_copy(z_in.at[:, pl.ds(pl.multiple_of(q * ROWS, ROWS), ROWS)], y_in.at[q], own_sem.at[0])
+    mine.start()
+    for i in range(7):
+        piece = z_in.at[:, pl.ds(pl.multiple_of(q_at[i] * ROWS, ROWS), ROWS)]
+        launch(remote(piece, y_in.at[q], y_send.at[i], y_recv.at[i], q_peers[i]))
+    mine.wait()
+    for i in range(7):
+        here = y_in.at[lax.rem(q + 7 - i, 8)]
+        remote(here, here, y_send.at[i], y_recv.at[i], q_peers[i]).wait_recv()
 
     lane = lax.broadcasted_iota(jnp.int32, (1, 128), 1)
+    tiles = [y_in[g].reshape(256, 128).astype(jnp.float32) for g in range(8)]
+    for pair_at in range(4):
+        both = [tiles[2 * pair_at][:, :P_SIZE], tiles[2 * pair_at + 1][:, :P_SIZE]]
+        padded[16:, pair_at * 128:(pair_at + 1) * 128] = jnp.concatenate(both, axis=1)
+    padded[16:, 512:640] = jnp.concatenate([tile[:, 64:80] for tile in tiles], axis=1)
+    padded[16:, 640:768] = jnp.concatenate([tile[:, 80:96] for tile in tiles], axis=1)
+    edge[0] = padded[256:272, :].astype(jnp.bfloat16)
+    launch(remote(edge.at[0], edge.at[1], halo_send, halo_recv, seq_next), s < 31)
+    logits = jnp.zeros((256, 128), jnp.float32)
+    for g in range(8):
+        logits = jnp.where(lane == g, tiles[g][:, 96:97] + tiles[g][:, 97:98], logits)
+    dt_buf[...] = logits
 
     def row_of(ref):
         row = jnp.zeros((1, 128), jnp.float32)
@@ -371,8 +392,8 @@
             decay = decay * fade
         return before, before_decay, state, decay
 
-    y_peers = [nexts["y"], y_far, prevs["y"]]
-    x_peers = [nexts["x"], x_far, prevs["x"]]
+    y_peers = [y_next, y_far, y_prev]
+    x_peers = [x_next, x_far, x_prev]
     level(0, y_state, y_decay, y, decay_1 * state_0 + state_1, decay_0 * decay_1, y_peers)
     inside(0)
     before_y, before_y_decay, row_state, row_decay = gather(0, y_state, y_decay, y, y_peers)
@@ -413,12 +434,14 @@
         in_specs=[vmem, vmem, vmem, vmem, smem, smem, smem],
         out_specs=vmem,
         scratch_shapes=[
-            pltpu.VMEM((8, 2 * ROWS, 4096), bf16),
-            pltpu.VMEM((2, 4, 4, 128, WIDTH), bf16),
-            pltpu.VMEM((ROWS, 4096), bf16),
-            pltpu.VMEM((2, 64, WIDTH), bf16),
-            pltpu.VMEM((8, 2, ROWS, WIDTH), f32),
-            pltpu.VMEM((8, ROWS, WIDTH), f32),
+            pltpu.VMEM((4, 8, ROWS, 2048), bf16),
+            pltpu.VMEM((16, SHARE, 1024), bf16),
+            pltpu.VMEM((8, 4, 256, 128), bf16),
+            pltpu.VMEM((8, 256, 128), f32),
+            pltpu.VMEM((8, 3, 256, 128), bf16),
+            pltpu.VMEM((8, 256, 128), bf16),
+            pltpu.VMEM((8, 256, 128), bf16),
+            pltpu.VMEM((8, 8, ROWS, 128), bf16),
             pltpu.VMEM((16 + 256, 768), f32),
             pltpu.VMEM((2, 16, 768), bf16),
             pltpu.VMEM((256, 512), bf16),
@@ -437,8 +460,8 @@
             pltpu.VMEM((2, N, 256), bf16),
             pltpu.VMEM((N, 256), bf16),
             pltpu.VMEM((256, 128), f32),
-            dma((2, 7, 2)), dma((2, 7, 2)), dma(()), dma(()),
-            dma((2, 5, 4)), dma((2, 5, 4)), dma((2, 2)), dma((2, 2)), dma((2,)), dma((2,)), dma(()),
+            dma((3,)), dma((7,)), dma((7,)), dma((3, 2)), dma((3, 2)), dma((4,)), dma((4,)), dma((4,)), dma((4,)),
+            dma((2, 8, 2)), dma((2, 8, 2)), dma((8, 3)), dma((8, 3)), dma((8,)), dma((8,)), dma((7,)), dma((7,)),
             dma(()), dma(()), dma((2,)), dma((2,)), dma((2, 2, 3)), dma((2, 2, 3)), dma(()), dma(()),
         ],
         compiler_params=pltpu.CompilerParams(
@@ -464,8 +487,14 @@
 ):
     weight_x = sampled(proj_mean, proj_devs, swag_coef)
     weight_bc = sampled(bc_mean, bc_devs, swag_coef).reshape(128, 256)
-    padding = jnp.zeros((128, WIDTH - 768 - 8), jnp.bfloat16)
-    weight = jnp.concatenate([weight_x, weight_bc, dt_weight, padding], axis=1)
+    turned = weight_bc.T
+    parts = [
+        weight_x.T.reshape(8, 64, 128),
+        turned[:128].reshape(8, 16, 128),
+        turned[128:].reshape(8, 16, 128),
+        jnp.pad(dt_weight.T[:, None, :], ((0, 0), (0, 15), (0, 0))),
+    ]
+    weight = jnp.concatenate(parts, axis=1)
     return layer(tokens, weight, conv_proj, conv_bc, dt_bias, decay_rate, skip_gain)
 
 

time: 148 us -> 122 us (0.82)
  Pallas kernels: 138 us -> 113 us
    pallas_call x1, Pallas kernels: 138 us -> 113 us  [layer(): pl.pallas_call(layer_kernel, out_shape=jax.ShapeDtypeStruct((256, 512), b...]
where the time goes in v3:
time: 122 us
  Pallas kernels  113 us (93%)
  local copies, waits for them, and re-layouts  4.68 us (4%)
  between operations  2.57 us (2%)
  other arithmetic  2.04 us (2%)
    pallas_call x1, Pallas kernels, layer(): pl.pallas_call(layer_kernel, out_shape=jax.ShapeDtypeStruct((256, 512), b...  113 us
    unnamed x7, local copies, waits for them, and re-layouts  3.07 us

profile of v3, /device:TPU:1, one launch (start us, length us, event | category | flops | bytes accessed | tf_op | source)
XLA Modules:
  0.0 122.0 jit_solution(13686048428624874156)
XLA Ops:
  0.0 0.0 copy-start.2
  0.0 0.0 copy-start
  0.0 0.7 copy-done.2
  0.7 0.7 fusion.6
  3.8 0.7 copy.17
  4.5 1.2 fusion.4
  5.7 0.0 copy-start.1
  5.8 0.1 copy.18
  5.9 0.0 copy-done
  5.9 0.7 copy-done.1
  6.7 0.1 fusion.3
  6.8 0.1 copy.15
  6.9 0.7 fusion.2.w_ref
  7.6 112.8 %layer.1 = bf16[256,512]{1,0:T(8,128)(2,1)} custom-call(bf16[32,8192]{1,0:T(8,128)(2,1)} %tok_ref.1, bf16[8,112,128]{2,1,0:T(8,128)(2,1)} %fusion.2.w_ref, f32[4,512]{1,0:T(4,128)} %conv_x_ref.1, f32[4,2,128]{2,1,0:T(2,128)} %conv_bc_ref.1, f32[8]{0:T(128)} %bias_ref.1, f32[8]{0:T(128)} %rate_ref.1, f32[8]{0:T(128)} %skip_ref.1), custom_call_target="tpu_custom_call" | custom-call | tf_op jit(solution)/shard_map/layer/pallas_call | solution.py:431
  120.4 1.7 %copy.20 = bf16[256,512]{1,0:T(8,128)(2,1)} copy(bf16[256,512]{1,0:T(8,128)(2,1)} %layer.1) | data formatting | bytes 524288
  (1 shorter events, 0.0 us)
Async XLA Ops:
  0.0 0.7 copy-start.2
  0.0 5.9 %copy-start = (bf16[4,128,512]{2,1,0:T(8,128)(2,1)S(1)}, bf16[4,128,512]{2,1,0:T(8,128)(2,1)}, u32[]{:S(2)}) copy-start(bf16[4,128,512]{2,1,0:T(8,128)(2,1)} %param.14) | copy-start | bytes 1572868
  5.7 0.9 copy-start.1

commit v4 on v3

--- a/solution.py
+++ b/solution.py
@@ -12,13 +12,15 @@
 MESH = pl.DeviceIdType.MESH
 SHARE = 112
 ROWS = 32
-
-
-def sampled(mean_part, dev_part, swag_coef):
-    factor = (2.0 * (dev_part.shape[0] - 1)) ** (-0.5)
-    accum = mean_part.astype(jnp.float32)
-    for member in range(dev_part.shape[0]):
-        accum = accum + factor * swag_coef[member] * dev_part[member].astype(jnp.float32)
+GROUPS_AT = (slice(0, 5), slice(5, 8))
+ORDER = (4, 3, 5, 2, 6, 1, 7, 0)
+
+
+def sampled(mean, devs, coef_ref):
+    factor = (2.0 * (len(devs) - 1)) ** (-0.5)
+    accum = mean.astype(jnp.float32)
+    for member, dev in enumerate(devs):
+        accum = accum + factor * coef_ref[member] * dev.astype(jnp.float32)
     return accum.astype(jnp.bfloat16)
 
 
@@ -38,20 +40,20 @@
 
 def fold(tile):
     lane = lax.broadcasted_iota(jnp.int32, tile.shape, 1)
-    joined = jnp.where(lane == 96, tile + pltpu.roll(tile, 127, 1), tile)
-    return jnp.where(lane == 97, 0.0, joined)
+    joined = jnp.where((lane >= 96) & (lane < 104), tile + pltpu.roll(tile, 120, 1), tile)
+    return jnp.where(lane >= 104, 0.0, joined)
 
 
 def pack(tile):
     lane = lax.broadcasted_iota(jnp.int32, tile.shape, 1)
     high = tile.astype(jnp.bfloat16).astype(jnp.float32)
-    low = pltpu.roll(tile - high, 1, 1)
-    return jnp.where(lane == 97, low, high).astype(jnp.bfloat16)
+    low = pltpu.roll(tile - high, 8, 1)
+    return jnp.where((lane >= 104) & (lane < 112), low, high).astype(jnp.bfloat16)
 
 
 def layer_kernel(
-    tok_ref, w_ref, conv_x_ref, conv_bc_ref, bias_ref, rate_ref, skip_ref, out_ref,
-    x_buf, ring, rs_out, rs_own, rs_in, z_out, z_in, y_in, padded, edge, values, keys, reads, inner, states,
+    tok_ref, mean_ref, devs_ref, bc_mean_ref, bc_devs_ref, dt_ref, coef_ref, conv_x_ref, conv_bc_ref, bias_ref, rate_ref, skip_ref, out_ref,
+    x_buf, w_ref, ring, rs_out, rs_own, rs_in, z_out, z_in, y_in, padded, edge, values, keys, reads, inner, states,
     pair_state, pair_decay, y_state, y_decay, x_state, x_decay, give_state, give_decay, inflow, outflow, dt_buf,
     own_sem, p_send, p_recv, a_send, a_recv, u_send, u_recv, c_send, c_recv, r_send, r_recv, rs_send, rs_recv,
     z_send, z_recv, y_send, y_recv,
@@ -86,6 +88,7 @@
     t_peers = [(f, s, at) for at in t_at]
     seq_next, seq_prev = (f, lax.min(s + 1, 31), t), (f, lax.max(s - 1, 0), t)
 
+    ring[:, 96:, :] = jnp.zeros((16, SHARE - 96, 1024), jnp.bfloat16)
     barrier = pltpu.get_barrier_semaphore()
     for peer in (x_next, x_far, x_prev, z_next, z_prev, *q_peers, *t_peers[1:]):
         pl.semaphore_signal(barrier, inc=1, device_id=peer, device_id_type=MESH)
@@ -122,10 +125,25 @@
     locals_ = [
         pltpu.make_async_copy(token_columns(half, x), token_place(half, x, q), own_sem.at[half]) for half in range(2)
     ]
+    for copy in locals_:
+        copy.start()
+    for tile in range(4):
+        columns = slice(tile * 128, (tile + 1) * 128)
+        weight = sampled(mean_ref[:, columns], [devs_ref[m, :, columns] for m in range(4)], coef_ref)
+        turned = weight.astype(jnp.float32).T.astype(jnp.bfloat16)
+        w_ref[2 * tile, :64, :] = turned[:64]
+        w_ref[2 * tile + 1, :64, :] = turned[64:]
+    for kind in range(2):
+        weight = sampled(bc_mean_ref[:, kind, :], [bc_devs_ref[m, :, kind, :] for m in range(4)], coef_ref)
+        turned = weight.astype(jnp.float32).T.astype(jnp.bfloat16)
+        for g in range(8):
+            w_ref[g, 64 + 16 * kind:80 + 16 * kind, :] = turned[16 * g:16 * g + 16]
+    dt_rows = jnp.concatenate([dt_ref[...].astype(jnp.float32), jnp.zeros((8, 128), jnp.float32)], axis=0)
+    for g in range(8):
+        w_ref[g, 96:, :] = dt_rows.astype(jnp.bfloat16)
     lanes = pl.ds(pl.multiple_of(q * 128, 128), 128)
     locals_.append(pltpu.make_async_copy(w_ref.at[q], ring.at[z, :, lanes], own_sem.at[2]))
-    for copy in locals_:
-        copy.start()
+    locals_[2].start()
     pl.semaphore_wait(barrier, 19 + jnp.where(s > 0, 1, 0) + jnp.where(s < 31, 1, 0))
 
     for i in range(7):
@@ -136,21 +154,30 @@
                 token_columns(half, wrap(x + 1 + i)), token_place(half, x, q), a_send.at[i, half], a_recv.at[i, half], peer
             ))
 
-    pieces = (pl.ds(0, 48), pl.ds(48, 64))
+    pieces = (pl.ds(0, 48), pl.ds(48, 48), pl.ds(96, 16))
 
     def ring_copy(way, k, b, slot):
         piece = ring.at[lax.rem(slot + 32, 16), pieces[b]]
         return remote(piece, piece, r_send.at[way, k, b], r_recv.at[way, k, b], z_next if way == 0 else z_prev)
 
+    def steps_here(slot):
+        return lax.rem(slot + 32, 8) == q
+
     def ring_send(k, b):
         for way in range(2):
+            slot = z - k if way == 0 else z + k
             if k < 7 or way == b:
-                launch(ring_copy(way, k, b, z - k if way == 0 else z + k))
+                launch(ring_copy(way, k, b, slot))
+            if b == 1 and (k < 7 or way == 0):
+                launch(ring_copy(way, k, 2, slot), steps_here(slot))
 
     def ring_wait(k, b):
         for way in range(2):
+            slot = z - 1 - k if way == 0 else z + 1 + k
             if k < 7 or way == b:
-                ring_copy(way, k, b, z - 1 - k if way == 0 else z + 1 + k).wait_recv()
+                ring_copy(way, k, b, slot).wait_recv()
+            if b == 1 and (k < 7 or way == 0):
+                pl.when(steps_here(slot))(ring_copy(way, k, 2, slot).wait_recv)
 
     def ring_step(k):
         for b in range(2):
@@ -224,10 +251,28 @@
             total = total + rs_in[by, i].astype(jnp.float32)
         packed = pack(fold(total))
         if by == 0:
-            z_in[t] = packed
+            z_in[ORDER.index(by)] = packed
         else:
             z_out[by] = packed
-            launch(remote(z_out.at[by], z_in.at[t], z_send.at[by], z_recv.at[by], t_peers[by]))
+            launch(remote(z_out.at[by], z_in.at[ORDER.index(by)], z_send.at[by], z_recv.at[by], t_peers[by]))
+
+    def spread_copy(group, i):
+        slots = GROUPS_AT[group]
+        owner = q if i == 7 else q_at[i]
+        piece = z_in.at[slots, pl.ds(pl.multiple_of(owner * ROWS, ROWS), ROWS)]
+        there = y_in.at[q, slots]
+        if i == 7:
+            return pltpu.make_async_copy(piece, there, own_sem.at[group])
+        return remote(piece, there, y_send.at[group, i], y_recv.at[group, i], q_peers[i])
+
+    def spread(group):
+        for by in ORDER[GROUPS_AT[group]]:
+            if by:
+                here = z_in.at[ORDER.index(by)]
+                remote(here, here, z_send.at[by], z_recv.at[by], t_peers[by]).wait_recv()
+        spread_copy(group, 7).start()
+        for i in range(7):
+            launch(spread_copy(group, i))
 
     multiply(4)
     ring_step(5)
@@ -249,32 +294,29 @@
     settle(1)
     settle(7)
     settle(0)
-    for by in range(1, 8):
-        here = z_in.at[lax.rem(t + 8 - by, 8)]
-        remote(here, here, z_send.at[by], z_recv.at[by], t_peers[by]).wait_recv()
-    mine = pltpu.make_async_copy(z_in.at[:, pl.ds(pl.multiple_of(q * ROWS, ROWS), ROWS)], y_in.at[q], own_sem.at[0])
-    mine.start()
-    for i in range(7):
-        piece = z_in.at[:, pl.ds(pl.multiple_of(q_at[i] * ROWS, ROWS), ROWS)]
-        launch(remote(piece, y_in.at[q], y_send.at[i], y_recv.at[i], q_peers[i]))
-    mine.wait()
-    for i in range(7):
-        here = y_in.at[lax.rem(q + 7 - i, 8)]
-        remote(here, here, y_send.at[i], y_recv.at[i], q_peers[i]).wait_recv()
+    spread(0)
+    spread(1)
+    for group in range(2):
+        spread_copy(group, 7).wait()
+        for i in range(7):
+            slots = GROUPS_AT[group]
+            here = y_in.at[lax.rem(q + 7 - i, 8), slots]
+            remote(here, here, y_send.at[group, i], y_recv.at[group, i], q_peers[i]).wait_recv()
 
     lane = lax.broadcasted_iota(jnp.int32, (1, 128), 1)
-    tiles = [y_in[g].reshape(256, 128).astype(jnp.float32) for g in range(8)]
-    for pair_at in range(4):
-        both = [tiles[2 * pair_at][:, :P_SIZE], tiles[2 * pair_at + 1][:, :P_SIZE]]
-        padded[16:, pair_at * 128:(pair_at + 1) * 128] = jnp.concatenate(both, axis=1)
-    padded[16:, 512:640] = jnp.concatenate([tile[:, 64:80] for tile in tiles], axis=1)
-    padded[16:, 640:768] = jnp.concatenate([tile[:, 80:96] for tile in tiles], axis=1)
+    for at, by in enumerate(ORDER):
+        first_row = pl.multiple_of(lax.rem(t + 8 - by, 8) * ROWS, ROWS)
+        rows = pl.ds(16 + first_row, ROWS)
+        tiles = [y_in[g, at].astype(jnp.float32) for g in range(8)]
+        for pair_at in range(4):
+            both = [tiles[2 * pair_at][:, :P_SIZE], tiles[2 * pair_at + 1][:, :P_SIZE]]
+            padded[rows, pair_at * 128:(pair_at + 1) * 128] = jnp.concatenate(both, axis=1)
+        padded[rows, 512:640] = jnp.concatenate([tile[:, 64:80] for tile in tiles], axis=1)
+        padded[rows, 640:768] = jnp.concatenate([tile[:, 80:96] for tile in tiles], axis=1)
+        logits = y_in[t, at].astype(jnp.float32)
+        dt_buf[pl.ds(first_row, ROWS), :] = pltpu.roll(logits, 32, 1) + pltpu.roll(logits, 24, 1)
     edge[0] = padded[256:272, :].astype(jnp.bfloat16)
     launch(remote(edge.at[0], edge.at[1], halo_send, halo_recv, seq_next), s < 31)
-    logits = jnp.zeros((256, 128), jnp.float32)
-    for g in range(8):
-        logits = jnp.where(lane == g, tiles[g][:, 96:97] + tiles[g][:, 97:98], logits)
-    dt_buf[...] = logits
 
     def row_of(ref):
         row = jnp.zeros((1, 128), jnp.float32)
@@ -423,7 +465,7 @@
             pl.when(condition)(copy.wait_send)
 
 
-def layer(tokens, weight, conv_x, conv_bc, bias, rate, skip):
+def layer(*operands):
     vmem = pl.BlockSpec(memory_space=pltpu.VMEM)
     smem = pl.BlockSpec(memory_space=pltpu.SMEM)
     dma = pltpu.SemaphoreType.DMA
@@ -431,10 +473,11 @@
     return pl.pallas_call(
         layer_kernel,
         out_shape=jax.ShapeDtypeStruct((256, 512), bf16),
-        in_specs=[vmem, vmem, vmem, vmem, smem, smem, smem],
+        in_specs=[vmem] * 6 + [smem, vmem, vmem, smem, smem, smem],
         out_specs=vmem,
         scratch_shapes=[
             pltpu.VMEM((4, 8, ROWS, 2048), bf16),
+            pltpu.VMEM((8, SHARE, 128), bf16),
             pltpu.VMEM((16, SHARE, 1024), bf16),
             pltpu.VMEM((8, 4, 256, 128), bf16),
             pltpu.VMEM((8, 256, 128), f32),
@@ -461,14 +504,14 @@
             pltpu.VMEM((N, 256), bf16),
             pltpu.VMEM((256, 128), f32),
             dma((3,)), dma((7,)), dma((7,)), dma((3, 2)), dma((3, 2)), dma((4,)), dma((4,)), dma((4,)), dma((4,)),
-            dma((2, 8, 2)), dma((2, 8, 2)), dma((8, 3)), dma((8, 3)), dma((8,)), dma((8,)), dma((7,)), dma((7,)),
+            dma((2, 8, 3)), dma((2, 8, 3)), dma((8, 3)), dma((8, 3)), dma((8,)), dma((8,)), dma((2, 7)), dma((2, 7)),
             dma(()), dma(()), dma((2,)), dma((2,)), dma((2, 2, 3)), dma((2, 2, 3)), dma(()), dma(()),
         ],
         compiler_params=pltpu.CompilerParams(
             collective_id=0, has_side_effects=True, vmem_limit_bytes=56 * 2**20
         ),
         name="layer",
-    )(tokens, weight, conv_x, conv_bc, bias, rate, skip)
+    )(*operands)
 
 
 def body(
@@ -485,17 +528,10 @@
     conv_proj,
     conv_bc,
 ):
-    weight_x = sampled(proj_mean, proj_devs, swag_coef)
-    weight_bc = sampled(bc_mean, bc_devs, swag_coef).reshape(128, 256)
-    turned = weight_bc.T
-    parts = [
-        weight_x.T.reshape(8, 64, 128),
-        turned[:128].reshape(8, 16, 128),
-        turned[128:].reshape(8, 16, 128),
-        jnp.pad(dt_weight.T[:, None, :], ((0, 0), (0, 15), (0, 0))),
-    ]
-    weight = jnp.concatenate(parts, axis=1)
-    return layer(tokens, weight, conv_proj, conv_bc, dt_bias, decay_rate, skip_gain)
+    return layer(
+        tokens, proj_mean, proj_devs, bc_mean, bc_devs, dt_weight.T, swag_coef,
+        conv_proj, conv_bc, dt_bias, decay_rate, skip_gain,
+    )
 
 
 def solution(mesh):

time: 122 us -> 111 us (0.910)
  Pallas kernels: 113 us -> 109 us
  local copies, waits for them, and re-layouts: 4.68 us -> 1.67 us
  between operations: 2.57 us -> 0.01 us
  other arithmetic: 2.04 us -> 0 us
    pallas_call x1, Pallas kernels: 113 us -> 109 us  [layer(): pl.pallas_call(layer_kernel, out_shape=jax.ShapeDtypeStruct((256, 512), b...]
    unnamed x7 -> x1, local copies, waits for them, and re-layouts: 3.07 us -> 1.67 us
where the time goes in v4:
time: 111 us
  Pallas kernels  109 us (98%)
  local copies, waits for them, and re-layouts  1.67 us (2%)
    pallas_call x1, Pallas kernels, layer(): pl.pallas_call(layer_kernel, out_shape=jax.ShapeDtypeStruct((256, 512), b...  109 us

profile of v4, /device:TPU:1, one launch (start us, length us, event | category | flops | bytes accessed | tf_op | source)
XLA Modules:
  0.0 110.9 jit_solution(16789200014285041561)
XLA Ops:
  0.0 109.2 %layer.1 = bf16[256,512]{1,0:T(8,128)(2,1)} custom-call(bf16[32,8192]{1,0:T(8,128)(2,1)} %tok_ref.1, bf16[128,512]{1,0:T(8,128)(2,1)} %mean_ref.1, bf16[4,128,512]{2,1,0:T(8,128)(2,1)} %devs_ref.1, bf16[128,2,128]{2,1,0:T(2,128)(2,1)} %bc_mean_ref.1, bf16[4,128,2,128]{3,2,1,0:T(2,128)(2,1)} %bc_devs_ref.1, bf16[8,128]{1,0:T(8,128)(2,1)} %bitcast.1, ...), custom_call_target="tpu_custom_call" | custom-call | tf_op jit(solution)/shard_map/layer/pallas_call | solution.py:473
  109.2 1.7 %copy.14 = bf16[256,512]{1,0:T(8,128)(2,1)} copy(bf16[256,512]{1,0:T(8,128)(2,1)} %layer.1) | data formatting | bytes 524288

commit v5 on v4

--- a/solution.py
+++ b/solution.py
@@ -12,7 +12,7 @@
 MESH = pl.DeviceIdType.MESH
 SHARE = 112
 ROWS = 32
-GROUPS_AT = (slice(0, 5), slice(5, 8))
+GROUPS_AT = (slice(0, 3), slice(3, 5), slice(5, 8))
 ORDER = (4, 3, 5, 2, 6, 1, 7, 0)
 
 
@@ -225,35 +225,50 @@
         here = unit(y_by, 1 - core)
         remote(here, here, c_send.at[index], c_recv.at[index], sibling).wait_recv()
 
-    def multiply(by):
-        tau = t_at[by]
+    def narrowed(by, tile, where_to, joined):
+        steps = q == t_at[by]
+
+        @pl.when(steps)
+        def _():
+            where_to[...] = pack(fold(tile) if joined else tile)
+
+        @pl.when(jnp.logical_not(steps))
+        def _():
+            where_to[...] = tile.astype(jnp.bfloat16)
+
+    def multiply(*bys):
         for owner in range(4):
-            total = jnp.zeros((256, SHARE), jnp.float32)
+            total = None
             for half in range(2):
-                total = total + lax.dot_general(
-                    x_buf[owner, :, :, half * 1024:(half + 1) * 1024].reshape(256, 1024), ring[tau + 8 * half],
-                    (((1,), (1,)), ((), ())), preferred_element_type=jnp.float32,
+                weight = jnp.concatenate([ring[t_at[by] + 8 * half] for by in bys], axis=0)
+                units = x_buf[owner, :, :, half * 1024:(half + 1) * 1024].reshape(256, 1024)
+                one = lax.dot_general(
+                    units, weight, (((1,), (1,)), ((), ())), preferred_element_type=jnp.float32
                 )
-            total = jnp.concatenate([total, jnp.zeros((256, 128 - SHARE), jnp.float32)], axis=1)
-            rs_out[by, owner] = pack(total)
-
-            @pl.when(x == owner)
-            def _():
-                rs_own[by] = total
-
-        for i, peer in enumerate((x_next, x_far, x_prev)):
-            launch(remote(rs_out.at[by, wrap(x + 1 + i)], rs_in.at[by, i], rs_send.at[by, i], rs_recv.at[by, i], peer))
+                total = one if total is None else total + one
+            for at, by in enumerate(bys):
+                tile = jnp.concatenate(
+                    [total[:, at * SHARE:(at + 1) * SHARE], jnp.zeros((256, 128 - SHARE), jnp.float32)], axis=1
+                )
+                narrowed(by, tile, rs_out.at[by, owner], False)
+
+                @pl.when(x == owner)
+                def _():
+                    rs_own[by] = tile
+
+        for by in bys:
+            for i, peer in enumerate((x_next, x_far, x_prev)):
+                launch(remote(rs_out.at[by, wrap(x + 1 + i)], rs_in.at[by, i], rs_send.at[by, i], rs_recv.at[by, i], peer))
 
     def settle(by):
         total = rs_own[by]
         for i, peer in enumerate((x_next, x_far, x_prev)):
             remote(rs_in.at[by, i], rs_in.at[by, i], rs_send.at[by, i], rs_recv.at[by, i], peer).wait_recv()
             total = total + rs_in[by, i].astype(jnp.float32)
-        packed = pack(fold(total))
         if by == 0:
-            z_in[ORDER.index(by)] = packed
+            narrowed(by, total, z_in.at[ORDER.index(by)], True)
         else:
-            z_out[by] = packed
+            narrowed(by, total, z_out.at[by], True)
             launch(remote(z_out.at[by], z_in.at[ORDER.index(by)], z_send.at[by], z_recv.at[by], t_peers[by]))
 
     def spread_copy(group, i):
@@ -275,17 +290,14 @@
             launch(spread_copy(group, i))
 
     multiply(4)
+    multiply(3, 5)
     ring_step(5)
-    multiply(3)
-    multiply(5)
+    multiply(2, 6)
     settle(4)
     ring_step(6)
-    multiply(2)
-    multiply(6)
     settle(3)
     settle(5)
-    multiply(1)
-    multiply(7)
+    multiply(1, 7)
     settle(2)
     settle(6)
     ring_wait(7, 0)
@@ -293,10 +305,11 @@
     multiply(0)
     settle(1)
     settle(7)
+    spread(0)
     settle(0)
-    spread(0)
     spread(1)
-    for group in range(2):
+    spread(2)
+    for group in range(3):
         spread_copy(group, 7).wait()
         for i in range(7):
             slots = GROUPS_AT[group]
@@ -504,7 +517,7 @@
             pltpu.VMEM((N, 256), bf16),
             pltpu.VMEM((256, 128), f32),
             dma((3,)), dma((7,)), dma((7,)), dma((3, 2)), dma((3, 2)), dma((4,)), dma((4,)), dma((4,)), dma((4,)),
-            dma((2, 8, 3)), dma((2, 8, 3)), dma((8, 3)), dma((8, 3)), dma((8,)), dma((8,)), dma((2, 7)), dma((2, 7)),
+            dma((2, 8, 3)), dma((2, 8, 3)), dma((8, 3)), dma((8, 3)), dma((8,)), dma((8,)), dma((3, 7)), dma((3, 7)),
             dma(()), dma(()), dma((2,)), dma((2,)), dma((2, 2, 3)), dma((2, 2, 3)), dma(()), dma(()),
         ],
         compiler_params=pltpu.CompilerParams(

time: 111 us -> 113 us (1.018); the launches traced: 111 us -> 112 us
  no operation moved by 1% of the time
where the time goes in v5:
time: 113 us; the launch traced here: 112 us
  Pallas kernels  110 us (97%)
  local copies, waits for them, and re-layouts  1.67 us (1%)
    pallas_call x1, Pallas kernels, layer(): pl.pallas_call(layer_kernel, out_shape=jax.ShapeDtypeStruct((256, 512), b...  110 us

profile of v5, /device:TPU:1, one launch (start us, length us, event | category | flops | bytes accessed | tf_op | source)
XLA Modules:
  0.0 111.6 jit_solution(8049721607196745935)
XLA Ops:
  0.0 109.9 %layer.1 = bf16[256,512]{1,0:T(8,128)(2,1)} custom-call(bf16[32,8192]{1,0:T(8,128)(2,1)} %tok_ref.1, bf16[128,512]{1,0:T(8,128)(2,1)} %mean_ref.1, bf16[4,128,512]{2,1,0:T(8,128)(2,1)} %devs_ref.1, bf16[128,2,128]{2,1,0:T(2,128)(2,1)} %bc_mean_ref.1, bf16[4,128,2,128]{3,2,1,0:T(2,128)(2,1)} %bc_devs_ref.1, bf16[8,128]{1,0:T(8,128)(2,1)} %bitcast.1, ...), custom_call_target="tpu_custom_call" | custom-call | tf_op jit(solution)/shard_map/layer/pallas_call | solution.py:486
  109.9 1.7 %copy.14 = bf16[256,512]{1,0:T(8,128)(2,1)} copy(bf16[256,512]{1,0:T(8,128)(2,1)} %layer.1) | data formatting | bytes 524288

commit v6 on v5

--- a/solution.py
+++ b/solution.py
@@ -12,7 +12,7 @@
 MESH = pl.DeviceIdType.MESH
 SHARE = 112
 ROWS = 32
-GROUPS_AT = (slice(0, 3), slice(3, 5), slice(5, 8))
+GROUPS_AT = (slice(0, 1), slice(1, 3), slice(3, 5), slice(5, 7), slice(7, 8))
 ORDER = (4, 3, 5, 2, 6, 1, 7, 0)
 
 
@@ -53,10 +53,10 @@
 
 def layer_kernel(
     tok_ref, mean_ref, devs_ref, bc_mean_ref, bc_devs_ref, dt_ref, coef_ref, conv_x_ref, conv_bc_ref, bias_ref, rate_ref, skip_ref, out_ref,
-    x_buf, w_ref, ring, rs_out, rs_own, rs_in, z_out, z_in, y_in, padded, edge, values, keys, reads, inner, states,
+    x_buf, w_ref, ring, rs_out, rs_own, rs_in, y_out, y_in, z_out, z_in, padded, edge, values, keys, reads, inner, states,
     pair_state, pair_decay, y_state, y_decay, x_state, x_decay, give_state, give_decay, inflow, outflow, dt_buf,
     own_sem, p_send, p_recv, a_send, a_recv, u_send, u_recv, c_send, c_recv, r_send, r_recv, rs_send, rs_recv,
-    z_send, z_recv, y_send, y_recv,
+    z_send, z_recv, y_send, y_recv, spread_sem,
     halo_send, halo_recv, p1_send, p1_recv, p2_send, p2_recv, p4_send, p4_recv,
 ):
     f = lax.axis_index("fsdp")
@@ -265,71 +265,82 @@
         for i, peer in enumerate((x_next, x_far, x_prev)):
             remote(rs_in.at[by, i], rs_in.at[by, i], rs_send.at[by, i], rs_recv.at[by, i], peer).wait_recv()
             total = total + rs_in[by, i].astype(jnp.float32)
-        if by == 0:
-            narrowed(by, total, z_in.at[ORDER.index(by)], True)
-        else:
-            narrowed(by, total, z_out.at[by], True)
-            launch(remote(z_out.at[by], z_in.at[ORDER.index(by)], z_send.at[by], z_recv.at[by], t_peers[by]))
+        narrowed(by, total, y_out.at[ORDER.index(by)], True)
 
     def spread_copy(group, i):
         slots = GROUPS_AT[group]
         owner = q if i == 7 else q_at[i]
-        piece = z_in.at[slots, pl.ds(pl.multiple_of(owner * ROWS, ROWS), ROWS)]
-        there = y_in.at[q, slots]
+        piece = y_out.at[slots, pl.ds(pl.multiple_of(owner * ROWS, ROWS), ROWS)]
+        there = y_in.at[slots, q]
         if i == 7:
-            return pltpu.make_async_copy(piece, there, own_sem.at[group])
+            return pltpu.make_async_copy(piece, there, spread_sem.at[group])
         return remote(piece, there, y_send.at[group, i], y_recv.at[group, i], q_peers[i])
 
     def spread(group):
-        for by in ORDER[GROUPS_AT[group]]:
-            if by:
-                here = z_in.at[ORDER.index(by)]
-                remote(here, here, z_send.at[by], z_recv.at[by], t_peers[by]).wait_recv()
         spread_copy(group, 7).start()
         for i in range(7):
             launch(spread_copy(group, i))
+
+    lane = lax.broadcasted_iota(jnp.int32, (1, 128), 1)
+
+    def collect(group):
+        slots = GROUPS_AT[group]
+        spread_copy(group, 7).wait()
+        for i in range(7):
+            here = y_in.at[slots, lax.rem(q + 7 - i, 8)]
+            remote(here, here, y_send.at[group, i], y_recv.at[group, i], q_peers[i]).wait_recv()
+        for at in range(slots.start, slots.stop):
+            by = ORDER[at]
+            tiles = [y_in[at, g].astype(jnp.float32) for g in range(8)]
+            joined = [
+                jnp.concatenate([tiles[2 * j][:, :P_SIZE], tiles[2 * j + 1][:, :P_SIZE]], axis=1) for j in range(4)
+            ]
+            joined.append(jnp.concatenate([tile[:, 64:80] for tile in tiles], axis=1))
+            joined.append(jnp.concatenate([tile[:, 80:96] for tile in tiles], axis=1))
+            steps = pltpu.roll(y_in[at, t_at[by]].astype(jnp.float32), 32, 1)
+            joined.append(jnp.where(lane < 16, steps, 0.0))
+            whole = jnp.concatenate(joined, axis=1).astype(jnp.bfloat16)
+            if by == 0:
+                z_in[t] = whole
+            else:
+                z_out[at] = whole
+                launch(remote(z_out.at[at], z_in.at[t], z_send.at[by], z_recv.at[by], t_peers[by]))
 
     multiply(4)
     multiply(3, 5)
     ring_step(5)
     multiply(2, 6)
     settle(4)
+    spread(0)
     ring_step(6)
     settle(3)
     settle(5)
+    spread(1)
     multiply(1, 7)
+    collect(0)
     settle(2)
     settle(6)
+    spread(2)
     ring_wait(7, 0)
     ring_wait(7, 1)
     multiply(0)
+    collect(1)
     settle(1)
     settle(7)
-    spread(0)
+    spread(3)
+    collect(2)
     settle(0)
-    spread(1)
-    spread(2)
-    for group in range(3):
-        spread_copy(group, 7).wait()
-        for i in range(7):
-            slots = GROUPS_AT[group]
-            here = y_in.at[lax.rem(q + 7 - i, 8), slots]
-            remote(here, here, y_send.at[group, i], y_recv.at[group, i], q_peers[i]).wait_recv()
-
-    lane = lax.broadcasted_iota(jnp.int32, (1, 128), 1)
-    for at, by in enumerate(ORDER):
-        first_row = pl.multiple_of(lax.rem(t + 8 - by, 8) * ROWS, ROWS)
-        rows = pl.ds(16 + first_row, ROWS)
-        tiles = [y_in[g, at].astype(jnp.float32) for g in range(8)]
-        for pair_at in range(4):
-            both = [tiles[2 * pair_at][:, :P_SIZE], tiles[2 * pair_at + 1][:, :P_SIZE]]
-            padded[rows, pair_at * 128:(pair_at + 1) * 128] = jnp.concatenate(both, axis=1)
-        padded[rows, 512:640] = jnp.concatenate([tile[:, 64:80] for tile in tiles], axis=1)
-        padded[rows, 640:768] = jnp.concatenate([tile[:, 80:96] for tile in tiles], axis=1)
-        logits = y_in[t, at].astype(jnp.float32)
-        dt_buf[pl.ds(first_row, ROWS), :] = pltpu.roll(logits, 32, 1) + pltpu.roll(logits, 24, 1)
-    edge[0] = padded[256:272, :].astype(jnp.bfloat16)
+    spread(4)
+    collect(3)
+    collect(4)
+    for by in range(1, 8):
+        here = z_in.at[lax.rem(t + 8 - by, 8)]
+        remote(here, here, z_send.at[by], z_recv.at[by], t_peers[by]).wait_recv()
+    padded[16:, :] = z_in[:, :, :768].reshape(256, 768).astype(jnp.float32)
+    edge[0] = z_in[7, 16:, :768]
     launch(remote(edge.at[0], edge.at[1], halo_send, halo_recv, seq_next), s < 31)
+    logits = z_in[:, :, 768:].reshape(256, 128).astype(jnp.float32)
+    dt_buf[...] = logits + pltpu.roll(logits, 120, 1)
 
     def row_of(ref):
         row = jnp.zeros((1, 128), jnp.float32)
@@ -496,8 +507,9 @@
             pltpu.VMEM((8, 256, 128), f32),
             pltpu.VMEM((8, 3, 256, 128), bf16),
             pltpu.VMEM((8, 256, 128), bf16),
-            pltpu.VMEM((8, 256, 128), bf16),
             pltpu.VMEM((8, 8, ROWS, 128), bf16),
+            pltpu.VMEM((8, ROWS, 896), bf16),
+            pltpu.VMEM((8, ROWS, 896), bf16),
             pltpu.VMEM((16 + 256, 768), f32),
             pltpu.VMEM((2, 16, 768), bf16),
             pltpu.VMEM((256, 512), bf16),
@@ -517,7 +529,7 @@
             pltpu.VMEM((N, 256), bf16),
             pltpu.VMEM((256, 128), f32),
             dma((3,)), dma((7,)), dma((7,)), dma((3, 2)), dma((3, 2)), dma((4,)), dma((4,)), dma((4,)), dma((4,)),
-            dma((2, 8, 3)), dma((2, 8, 3)), dma((8, 3)), dma((8, 3)), dma((8,)), dma((8,)), dma((3, 7)), dma((3, 7)),
+            dma((2, 8, 3)), dma((2, 8, 3)), dma((8, 3)), dma((8, 3)), dma((8,)), dma((8,)), dma((5, 7)), dma((5, 7)), dma((5,)),
             dma(()), dma(()), dma((2,)), dma((2,)), dma((2, 2, 3)), dma((2, 2, 3)), dma(()), dma(()),
         ],
         compiler_params=pltpu.CompilerParams(

time: 113 us -> 109 us (0.965)
  Pallas kernels: 110 us -> 107 us
    pallas_call x1, Pallas kernels: 110 us -> 107 us  [layer(): pl.pallas_call(layer_kernel, out_shape=jax.ShapeDtypeStruct((256, 512), b...]
where the time goes in v6:
time: 109 us
  Pallas kernels  107 us (98%)
  local copies, waits for them, and re-layouts  1.67 us (2%)
    pallas_call x1, Pallas kernels, layer(): pl.pallas_call(layer_kernel, out_shape=jax.ShapeDtypeStruct((256, 512), b...  107 us

profile of v6, /device:TPU:1, one launch (start us, length us, event | category | flops | bytes accessed | tf_op | source)
XLA Modules:
  0.0 108.6 jit_solution(9027635677677558739)
XLA Ops:
  0.0 107.0 %layer.1 = bf16[256,512]{1,0:T(8,128)(2,1)} custom-call(bf16[32,8192]{1,0:T(8,128)(2,1)} %tok_ref.1, bf16[128,512]{1,0:T(8,128)(2,1)} %mean_ref.1, bf16[4,128,512]{2,1,0:T(8,128)(2,1)} %devs_ref.1, bf16[128,2,128]{2,1,0:T(2,128)(2,1)} %bc_mean_ref.1, bf16[4,128,2,128]{3,2,1,0:T(2,128)(2,1)} %bc_devs_ref.1, bf16[8,128]{1,0:T(8,128)(2,1)} %bitcast.1, ...), custom_call_target="tpu_custom_call" | custom-call | tf_op jit(solution)/shard_map/layer/pallas_call | solution.py:497
  107.0 1.7 %copy.14 = bf16[256,512]{1,0:T(8,128)(2,1)} copy(bf16[256,512]{1,0:T(8,128)(2,1)} %layer.1) | data formatting | bytes 524288

commit v7 on v6

--- a/solution.py
+++ b/solution.py
@@ -333,12 +333,16 @@
     spread(4)
     collect(3)
     collect(4)
-    for by in range(1, 8):
+    def arrived(by):
         here = z_in.at[lax.rem(t + 8 - by, 8)]
-        remote(here, here, z_send.at[by], z_recv.at[by], t_peers[by]).wait_recv()
-    padded[16:, :] = z_in[:, :, :768].reshape(256, 768).astype(jnp.float32)
+        remote(here, here, z_send.at[by], z_recv.at[by], z_next).wait_recv()
+
+    pl.when(t < 7)(lambda: arrived(lax.rem(t + 1, 8)))
     edge[0] = z_in[7, 16:, :768]
     launch(remote(edge.at[0], edge.at[1], halo_send, halo_recv, seq_next), s < 31)
+    for by in (4, 3, 5, 2, 6, 1, 7):
+        pl.when(t + 1 != by)(lambda by=by: arrived(by))
+    padded[16:, :] = z_in[:, :, :768].reshape(256, 768).astype(jnp.float32)
     logits = z_in[:, :, 768:].reshape(256, 128).astype(jnp.float32)
     dt_buf[...] = logits + pltpu.roll(logits, 120, 1)
 

time: 109 us -> 108 us (level)
  no operation moved by 1% of the time
where the time goes in v7:
time: 108 us
  Pallas kernels  106 us (98%)
  local copies, waits for them, and re-layouts  1.67 us (2%)
    pallas_call x1, Pallas kernels, layer(): pl.pallas_call(layer_kernel, out_shape=jax.ShapeDtypeStruct((256, 512), b...  106 us

profile of v7, /device:TPU:1, one launch (start us, length us, event | category | flops | bytes accessed | tf_op | source)
XLA Modules:
  0.0 108.2 jit_solution(14279223414298429085)
XLA Ops:
  0.0 106.5 %layer.1 = bf16[256,512]{1,0:T(8,128)(2,1)} custom-call(bf16[32,8192]{1,0:T(8,128)(2,1)} %tok_ref.1, bf16[128,512]{1,0:T(8,128)(2,1)} %mean_ref.1, bf16[4,128,512]{2,1,0:T(8,128)(2,1)} %devs_ref.1, bf16[128,2,128]{2,1,0:T(2,128)(2,1)} %bc_mean_ref.1, bf16[4,128,2,128]{3,2,1,0:T(2,128)(2,1)} %bc_devs_ref.1, bf16[8,128]{1,0:T(8,128)(2,1)} %bitcast.1, ...), custom_call_target="tpu_custom_call" | custom-call | tf_op jit(solution)/shard_map/layer/pallas_call | solution.py:501
  106.5 1.7 %copy.14 = bf16[256,512]{1,0:T(8,128)(2,1)} copy(bf16[256,512]{1,0:T(8,128)(2,1)} %layer.1) | data formatting | bytes 524288

commit v8 on v7

--- a/solution.py
+++ b/solution.py
@@ -415,13 +415,13 @@
     launch(remote(give_state.at[1 - core], pair_state, p1_send.at[0], p1_recv.at[0], sibling))
     launch(remote(give_decay.at[1 - core], pair_decay, p1_send.at[1], p1_recv.at[1], sibling))
 
-    def inside(b):
+    def inside(b, *pairs):
         here = slice(b * SPAN, (b + 1) * SPAN)
         scores = lax.dot_general(
             reads[here, :], keys[here, :], (((1,), (1,)), ((), ())), preferred_element_type=jnp.float32
         )
         masked = jnp.where(causal, scores, 0.0)
-        for pair_at in range(4):
+        for pair_at in pairs:
             both = []
             for head in (2 * pair_at, 2 * pair_at + 1):
                 gap = cums[b][:, head:head + 1] - cum_rows[b][head:head + 1, :]
@@ -432,6 +432,7 @@
                 ))
             inner[here, pair_at * 128:(pair_at + 1) * 128] = jnp.concatenate(both, axis=1)
 
+    inside(0, 0, 1)
     remote(give_state.at[1 - core], pair_state, p1_send.at[0], p1_recv.at[0], sibling).wait_recv()
     remote(give_decay.at[1 - core], pair_decay, p1_send.at[1], p1_recv.at[1], sibling).wait_recv()
     first = core == 0
@@ -465,16 +466,18 @@
     y_peers = [y_next, y_far, y_prev]
     x_peers = [x_next, x_far, x_prev]
     level(0, y_state, y_decay, y, decay_1 * state_0 + state_1, decay_0 * decay_1, y_peers)
-    inside(0)
+    inside(0, 2, 3)
+    inside(1, 0)
     before_y, before_y_decay, row_state, row_decay = gather(0, y_state, y_decay, y, y_peers)
     level(1, x_state, x_decay, x, row_state, row_decay, x_peers)
-    inside(1)
+    inside(1, 1, 2)
     before_x, _, _, _ = gather(1, x_state, x_decay, x, x_peers)
     into_0 = before_y_decay * before_x + before_y
     into_1 = decay_0 * into_0 + state_0
     outflow[...] = jnp.where(first, into_1, into_0).astype(jnp.bfloat16)
     launch(remote(outflow, inflow.at[core], p4_send, p4_recv, sibling))
     inflow[core] = jnp.where(first, into_0, into_1).astype(jnp.bfloat16)
+    inside(1, 3)
     remote(outflow, inflow.at[1 - core], p4_send, p4_recv, sibling).wait_recv()
     entering = jnp.concatenate([inflow[0], inflow[1]], axis=1)
     skips = expand(row_of(skip_ref))

time: 108 us -> 108 us (level)
  no operation moved by 1% of the time
where the time goes in v8:
time: 108 us
  Pallas kernels  107 us (99%)
  local copies, waits for them, and re-layouts  1.67 us (2%)
    pallas_call x1, Pallas kernels, layer(): pl.pallas_call(layer_kernel, out_shape=jax.ShapeDtypeStruct((256, 512), b...  107 us

profile of v8, /device:TPU:1, one launch (start us, length us, event | category | flops | bytes accessed | tf_op | source)
XLA Modules:
  0.0 108.2 jit_solution(16745718652190085888)
XLA Ops:
  0.0 106.5 %layer.1 = bf16[256,512]{1,0:T(8,128)(2,1)} custom-call(bf16[32,8192]{1,0:T(8,128)(2,1)} %tok_ref.1, bf16[128,512]{1,0:T(8,128)(2,1)} %mean_ref.1, bf16[4,128,512]{2,1,0:T(8,128)(2,1)} %devs_ref.1, bf16[128,2,128]{2,1,0:T(2,128)(2,1)} %bc_mean_ref.1, bf16[4,128,2,128]{3,2,1,0:T(2,128)(2,1)} %bc_devs_ref.1, bf16[8,128]{1,0:T(8,128)(2,1)} %bitcast.1, ...), custom_call_target="tpu_custom_call" | custom-call | tf_op jit(solution)/shard_map/layer/pallas_call | solution.py:504
  106.5 1.7 %copy.14 = bf16[256,512]{1,0:T(8,128)(2,1)} copy(bf16[256,512]{1,0:T(8,128)(2,1)} %layer.1) | data formatting | bytes 524288
